TPU v7x, 512 devices: a whole 4x8x8 slice. The times are simulated.
512 devices in a mesh: band: 32 (over x, y_hi, core), tm: 16 (over y_lo, z).
Axes of the slice: x: 4, y: 8 (y_hi: 4, y_lo: 2; y = y_hi * 2 + y_lo), z: 8, core: 2. Of those that a mesh axis runs over, the one named last changes fastest.
Arguments:
- partial_sums: float32 [4096, 16384], P('band', 'tm'), may hold values from -6 to 6
- delays: int32 [5, 4096], replicated, may hold values from 0 to 96, as said below
Outputs:
- best_snr: float32 [4096, 16384], P(None, ('tm', 'band'))
Inputs may be any that keep to these rules, and one draw needn't show every extreme that they name: Whole delays from the channel frequencies and a range of trial dispersion measures, never falling with the merged row within each subband; the top row of the last section has exactly 96.
All inputs are finite; a program needn't handle non-finite values.
Results may differ from a plain program's by a relative error of at most 0.00002.
Values sent between devices are 32-bit elements; how exact they have to be, the bound alone decides.
No kernel may reach another device: no remote copies, remote signals or barrier semaphores. Data moves between devices by JAX's collectives and lax.ppermute only.
A program may use at most 128 MiB of HBM per device.

v0:
```python
import math

import jax
import jax.numpy as jnp
import numpy as np
from jax import lax
from jax.sharding import PartitionSpec as P

HALO = 96
WMAX = 64


def partner(block, axis, apart):
    count = lax.axis_size(axis)
    route = []
    for low in range(count):
        high = low | 1 << apart
        if high != low and high < count:
            route += [(low, high), (high, low)]
    return lax.ppermute(block, axis, route)


def shifted(value, axis, steps):
    count = lax.axis_size(axis)
    initial, last = (max(0, -steps), min(count, count - steps))
    return lax.ppermute(value, axis, [(source, source + steps) for source in range(initial, last)])


def shifted_rows(row_data, delay_rows, length):

    def one_row(single_row, row_shift):
        return lax.dynamic_slice_in_dim(single_row, row_shift, length, 0)

    return jax.vmap(one_row)(row_data, delay_rows)


def boxcar_best(state_rows, time_len, band_count):
    box_sums = state_rows
    best_snr = box_sums[:, WMAX:] * (1.0 / math.sqrt(band_count))
    box_width = 1
    while box_width < WMAX:
        box_sums = box_sums[:, box_width:] + box_sums[:, :-box_width]
        box_width = box_width * 2
        best_snr = jnp.maximum(
            best_snr,
            box_sums[:, box_sums.shape[1] - time_len :] * (1.0 / math.sqrt(box_width * band_count)),
        )
    return best_snr


def body(partial_sums, delays):
    band_count = lax.axis_size("band")
    sections = band_count.bit_length() - 1
    rows_dev = partial_sums.shape[0]
    half_rows = rows_dev // 2
    my_band = lax.axis_index("band")
    state_rows = partial_sums
    block_index = jnp.int32(0)
    for section_idx in range(sections):
        group_size = 2 ** (section_idx + 1)
        upper_side = my_band >> section_idx & 1
        is_lower = upper_side == 0
        first_half = state_rows[:half_rows]
        second_half = state_rows[half_rows:]
        sending = jnp.where(is_lower, second_half, first_half)
        keeping = jnp.where(is_lower, first_half, second_half)
        arriving = partner(sending, "band", section_idx)
        lower_rows = jnp.where(is_lower, keeping, arriving)
        upper_rows = jnp.where(is_lower, arriving, keeping)
        block_index = 2 * block_index + upper_side
        row_start = (my_band >> section_idx + 1) * (rows_dev * group_size) + block_index * rows_dev
        shifts = lax.dynamic_slice_in_dim(delays[section_idx], row_start, rows_dev, 0)
        columns = state_rows.shape[1]
        rim_cols = shifted(lower_rows[:, :HALO], "tm", -1)
        extended = jnp.concatenate([lower_rows, rim_cols], axis=1)
        state_rows = jnp.repeat(upper_rows, 2, axis=0) + shifted_rows(
            jnp.repeat(extended, 2, axis=0), shifts, columns
        )
    time_len = state_rows.shape[1]
    tail_cols = shifted(state_rows[:, time_len - WMAX :], "tm", 1)
    box_sums = jnp.concatenate([tail_cols, state_rows], axis=1)
    best_snr = boxcar_best(box_sums, time_len, band_count)
    regrouped = lax.all_to_all(best_snr, "band", split_axis=1, concat_axis=0, tiled=True)
    slab_cols = regrouped.shape[1]
    sources = np.arange(band_count)
    block_order = np.zeros(band_count, dtype=np.int64)
    for bit_idx in range(sections):
        block_order = block_order + (sources >> bit_idx & 1) * (1 << sections - 1 - bit_idx)
    stacked = regrouped.reshape(band_count, rows_dev, slab_cols)
    return stacked[block_order].reshape(band_count * rows_dev, slab_cols)


def solution(mesh):
    in_specs = (P("band", "tm"), P())
    out_specs = P(None, ("tm", "band"))
    return jax.shard_map(body, mesh=mesh, in_specs=in_specs, out_specs=out_specs, check_vma=False)
```

profile of v0, /device:TPU:9, one launch (start us, length us, event | category | flops | bytes accessed | tf_op | source)
XLA Modules:
  0.0 1467.7 jit_solution(6284147238739243304)
XLA Ops:
  1.1 2.6 collective-permute-start
  4.9 10.6 collective-permute-start.1
  17.2 265.5 %while.5 = (s32[]{:T(128)}, f32[128,1120]{1,0:T(8,128)S(1)}, s32[128,2]{0,1:T(2,128)S(1)}, f32[128,1024]{1,0:T(8,128)S(1)}, s32[]{:T(128)}, /*index=5*/s32[]{:T(128)}) while((s32[]{:T(128)}, f32[128,1120]{1,0:T(8,128)S(1)}, s32[128,2]{0,1:T(2,128)S(1)}, f32[128,1024]{1,0:T(8,128)S(1)}, s32[]{:T(128)}, /*index=5*/s32[]{:T(128)}) %tuple.90), condition=%wide.while_cond, body=%wide.while_body.sunk | while | flops 2 | bytes 16497 | solution.py:32
  17.9 1.3 dynamic-slice.36
  20.0 1.3 dynamic-slice.36
  22.0 1.3 dynamic-slice.36
  24.1 1.3 dynamic-slice.36
  26.2 1.3 dynamic-slice.36
  28.3 1.3 dynamic-slice.36
  30.3 1.3 dynamic-slice.36
  32.4 1.3 dynamic-slice.36
  34.5 1.3 dynamic-slice.36
  282.8 4.2 collective-permute-start.2
  287.1 7.6 collective-permute-done.2
  294.8 7.9 collective-permute-start.3
  304.4 265.5 %while.6 = (s32[]{:T(128)}, f32[128,1120]{1,0:T(8,128)S(1)}, s32[128,2]{0,1:T(2,128)S(1)}, f32[128,1024]{1,0:T(8,128)S(1)}, s32[]{:T(128)}, /*index=5*/s32[]{:T(128)}) while((s32[]{:T(128)}, f32[128,1120]{1,0:T(8,128)S(1)}, s32[128,2]{0,1:T(2,128)S(1)}, f32[128,1024]{1,0:T(8,128)S(1)}, s32[]{:T(128)}, /*index=5*/s32[]{:T(128)}) %tuple.93), condition=%wide.while_cond.1, body=%wide.while_body.1.sunk | while | flops 2 | bytes 16497 | solution.py:32
  570.1 6.6 collective-permute-start.4
  576.6 12.1 collective-permute-done.4
  588.8 5.2 collective-permute-start.5
  595.6 265.5 %while.7 = (s32[]{:T(128)}, f32[128,1120]{1,0:T(8,128)S(1)}, s32[128,2]{0,1:T(2,128)S(1)}, f32[128,1024]{1,0:T(8,128)S(1)}, s32[]{:T(128)}, /*index=5*/s32[]{:T(128)}) while((s32[]{:T(128)}, f32[128,1120]{1,0:T(8,128)S(1)}, s32[128,2]{0,1:T(2,128)S(1)}, f32[128,1024]{1,0:T(8,128)S(1)}, s32[]{:T(128)}, /*index=5*/s32[]{:T(128)}) %tuple.96), condition=%wide.while_cond.2, body=%wide.while_body.2.sunk | while | flops 2 | bytes 16497 | solution.py:32
  861.2 3.1 collective-permute-start.6
  864.4 4.0 collective-permute-done.6
  868.4 5.8 collective-permute-start.7
  875.9 265.5 %while.8 = (s32[]{:T(128)}, f32[128,1120]{1,0:T(8,128)S(1)}, s32[128,2]{0,1:T(2,128)S(1)}, f32[128,1024]{1,0:T(8,128)S(1)}, s32[]{:T(128)}, /*index=5*/s32[]{:T(128)}) while((s32[]{:T(128)}, f32[128,1120]{1,0:T(8,128)S(1)}, s32[128,2]{0,1:T(2,128)S(1)}, f32[128,1024]{1,0:T(8,128)S(1)}, s32[]{:T(128)}, /*index=5*/s32[]{:T(128)}) %tuple.99), condition=%wide.while_cond.3, body=%wide.while_body.3.sunk | while | flops 2 | bytes 16497 | solution.py:32
  1141.5 4.7 collective-permute-start.8
  1146.2 4.0 collective-permute-done.8
  1150.2 5.8 collective-permute-start.9
  1157.7 265.5 %while.9 = (s32[]{:T(128)}, f32[128,1120]{1,0:T(8,128)S(1)}, s32[128,2]{0,1:T(2,128)S(1)}, f32[128,1024]{1,0:T(8,128)S(1)}, s32[]{:T(128)}, /*index=5*/s32[]{:T(128)}) while((s32[]{:T(128)}, f32[128,1120]{1,0:T(8,128)S(1)}, s32[128,2]{0,1:T(2,128)S(1)}, f32[128,1024]{1,0:T(8,128)S(1)}, s32[]{:T(128)}, /*index=5*/s32[]{:T(128)}) %tuple.102), condition=%wide.while_cond.4, body=%wide.while_body.4.sunk | while | flops 2 | bytes 16497 | solution.py:32
  1423.3 1.9 collective-permute-start.10
  1425.3 5.5 collective-permute-done.10
  1434.3 15.3 %all-to-all-start = ((f32[128,32,32]{0,2,1:T(8,128)}), f32[128,32,32]{0,2,1:T(8,128)S(1)}, u32[]{:S(2)}, u32[]{:S(2)}) async-start(f32[128,32,32]{0,2,1:T(8,128)} %bitcast.5), calls=%async_computation | async-start | bytes 1048576 | tf_op jit(solution)/shard_map/all_to_all | solution.py:83
  1449.7 16.6 %all-to-all-done = f32[128,32,32]{0,2,1:T(8,128)S(1)} async-done(((f32[128,32,32]{0,2,1:T(8,128)}), f32[128,32,32]{0,2,1:T(8,128)S(1)}, u32[]{:S(2)}, u32[]{:S(2)}) %all-to-all-start) | async-done | bytes 524320 | tf_op jit(solution)/shard_map/all_to_all | solution.py:83
  (2632 shorter events, 1316.5 us)
Async XLA Ops:
  0.0 4.9 copy-start
  0.0 3.7 copy-start.1
  1.1 3.7 collective-permute-start
  4.9 11.6 collective-permute-start.1
  282.8 11.9 collective-permute-start.2
  294.8 8.9 collective-permute-start.3
  570.1 18.6 %collective-permute-start.4 = (f32[64,1024]{1,0:T(8,128)S(1)}, f32[64,1024]{1,0:T(8,128)S(1)}, u32[]{:S(2)}, u32[]{:S(2)}) collective-permute-start(f32[64,1024]{1,0:T(8,128)S(1)} %slice_select_fusion.5), channel_id=1, source_target_pairs={{0,64},{64,0},{16,80},{80,16},{32,96},{96,32},{48,112},{112,48},{1... | collective-permute-start | bytes 786440 | tf_op jit(solution)/shard_map/ppermute | solution.py:20
  588.8 6.2 collective-permute-start.5
  861.2 7.1 collective-permute-start.6
  868.4 6.8 collective-permute-start.7
  1141.5 8.6 collective-permute-start.8
  1150.2 6.8 collective-permute-start.9
  1423.3 7.4 collective-permute-start.10
  1434.3 15.4 %copy-start.2 = (s32[32]{0:T(128)S(1)}, s32[32]{0:T(128)}, u32[]{:S(2)}) copy-start(s32[32]{0:T(128)} %constant.131) | copy-start | bytes 388
  1434.3 32.0 %all-to-all-start = ((f32[128,32,32]{0,2,1:T(8,128)}), f32[128,32,32]{0,2,1:T(8,128)S(1)}, u32[]{:S(2)}, u32[]{:S(2)}) async-start(f32[128,32,32]{0,2,1:T(8,128)} %bitcast.5), calls=%async_computation | async-start | bytes 1048576 | tf_op jit(solution)/shard_map/all_to_all | solution.py:83
where the time goes:
time: 1480 us; the launch traced here: 1470 us
  local copies, waits for them, and re-layouts  1320 us (89%)
  starting transfers between devices  73.5 us (5%)
  waiting for transfers between devices  52.9 us (4%)
  loops' own time  15.5 us (1%)
    gather x2560, local copies, waits for them, and re-layouts  1310 us
    ppermute x6, starting transfers between devices, shifted(): lax.ppermute(value, axis, [(source, source + steps) for source in range(i...  37.1 us
  transfers between devices with their start and end apart: 12, of which 12 were waited for; matrix products, arithmetic and copies ran while one was open for 0% of the time, Pallas kernels for 0%

commit v1 on v0

v1 whole, which is shorter than its diff:
```python
import functools
import math

import jax
import jax.numpy as jnp
from jax import lax
from jax.experimental import pallas as pl
from jax.experimental.pallas import tpu as pltpu
from jax.sharding import PartitionSpec as P

HALO = 96
WMAX = 64
LANES = 128
SLOTS = 16


def shifted(value, axis, steps):
    count = lax.axis_size(axis)
    initial, last = (max(0, -steps), min(count, count - steps))
    return lax.ppermute(value, axis, [(source, source + steps) for source in range(initial, last)])


def pack_kernel(sections, band_count, x_ref, delays_ref, out_ref, shifts_ref):
    rows, cols = x_ref.shape
    blocks = cols // LANES
    part = rows // band_count
    for chunk in range(band_count):
        for block in range(blocks):
            start = chunk * part * blocks + block * part
            out_ref[start : start + part, :] = x_ref[
                chunk * part : chunk * part + part, block * LANES : (block + 1) * LANES
            ]
    my_band = lax.axis_index("band")
    lane = lax.broadcasted_iota(jnp.int32, (1, LANES), 1)
    for section_idx in range(sections):
        group = 2 << section_idx
        span = part * group
        first = my_band * span
        line = jnp.zeros((1, LANES), jnp.int32)
        for merged in range(band_count // group):
            column = pl.multiple_of(merged * group * LANES + first // LANES * LANES, LANES)
            values = delays_ref[section_idx : section_idx + 1, pl.ds(column, LANES)]
            turn = lax.rem(merged * span - lax.rem(first, LANES) + LANES, LANES)
            values = pltpu.roll(values, turn, 1)
            line = jnp.where((lane >= merged * span) & (lane < (merged + 1) * span), values, line)
        shifts_ref[section_idx : section_idx + 1, :] = line


def pack(x, delays, sections, band_count):
    rows, cols = x.shape
    return pl.pallas_call(
        functools.partial(pack_kernel, sections, band_count),
        out_shape=[
            jax.ShapeDtypeStruct((rows * cols // LANES, LANES), x.dtype),
            jax.ShapeDtypeStruct((sections, LANES), jnp.int32),
        ],
        in_specs=[pl.BlockSpec(memory_space=pltpu.VMEM)] * 2,
        out_specs=[pl.BlockSpec(memory_space=pltpu.VMEM)] * 2,
        compiler_params=pltpu.CompilerParams(vmem_limit_bytes=16 * 2**20),
    )(x, delays)


def merge_kernel(sections, band_count, delays_ref, main_ref, right_ref, left_ref, out_ref, ping, pong, turned):
    rows = LANES
    part = rows // band_count
    blocks = main_ref.shape[0] // rows
    right_blocks = right_ref.shape[0] // rows
    left_blocks = left_ref.shape[0] // rows
    time_len = blocks * LANES
    lane = lax.broadcasted_iota(jnp.int32, (8, LANES), 1)
    slot = lax.broadcasted_iota(jnp.int32, (8, LANES), 0)
    last_slot = slot == 7

    def fill(row, _):
        chunk, local = row // part, lax.rem(row, part)
        ping[row, 0:blocks, :] = main_ref[pl.ds(chunk * blocks * part + local, blocks, stride=part), :]
        ping[row, blocks : blocks + right_blocks, :] = right_ref[
            pl.ds(chunk * right_blocks * part + local, right_blocks, stride=part), :
        ]
        ping[row, SLOTS - 1 : SLOTS, :] = left_ref[pl.ds((chunk * left_blocks + left_blocks - 1) * part + local, 1), :]
        return 0

    lax.fori_loop(0, rows, fill, 0, unroll=8)

    source, target = ping, pong
    for section_idx in range(sections):
        span = (rows // band_count) << (section_idx + 1)
        half = span // 2

        def merge(step, _, source=source, target=target, half=half, span=span, section_idx=section_idx):
            within = lax.rem(step, half)
            base = step * 2 - within * 2
            lower = base + within
            upper = lower + half
            low_a = source[lower, 0:8, :]
            low_b = source[lower, 8:16, :]
            up_a = source[upper, 0:8, :]
            up_b = source[upper, 8:16, :]
            roll_a = pltpu.roll(low_a, 7, 0)
            roll_b = pltpu.roll(low_b, 7, 0)
            next_a = jnp.where(last_slot, roll_b, roll_a)
            next_b = jnp.where(last_slot, roll_a, roll_b)
            for side in range(2):
                row = base + within * 2 + side
                delay = delays_ref[section_idx, row]
                turn = lax.rem(LANES - delay, LANES)
                own = lane >= delay
                target[row, 0:8, :] = up_a + pltpu.roll(jnp.where(own, low_a, next_a), turn, 1)
                target[row, 8:16, :] = up_b + pltpu.roll(jnp.where(own, low_b, next_b), turn, 1)
            return 0

        lax.fori_loop(0, rows // 2, merge, 0, unroll=8)
        source, target = target, source

    flat = source.reshape(rows * SLOTS, LANES)
    before = flat[pl.ds(SLOTS - 1, rows, stride=SLOTS), :].T
    keep = lax.axis_index("tm") > 0
    turned[0:WMAX, :] = jnp.where(keep, before[LANES - WMAX :, :], 0.0)
    for block in range(blocks):
        turned[WMAX + block * LANES : WMAX + (block + 1) * LANES, :] = flat[
            pl.ds(block, rows, stride=SLOTS), :
        ].T

    piece = 64

    def detect(index, _):
        start = pl.multiple_of(index * piece, piece)
        sums = turned[pl.ds(start, piece + WMAX), :]
        best = sums[WMAX:, :] * (1.0 / math.sqrt(band_count))
        width = 1
        while width < WMAX:
            sums = sums + pltpu.roll(sums, width, 0)
            width *= 2
            best = jnp.maximum(best, sums[WMAX:, :] * (1.0 / math.sqrt(width * band_count)))
        out_ref[pl.ds(start, piece), :] = best
        return 0

    lax.fori_loop(0, time_len // piece, detect, 0)


def body(partial_sums, delays):
    band_count = lax.axis_size("band")
    sections = band_count.bit_length() - 1
    rows, cols = partial_sums.shape
    blocks = cols // LANES
    part = rows // band_count
    packed, shifts = pack(partial_sums, delays, sections, band_count)
    mine = lax.all_to_all(packed.reshape(band_count, part * blocks, LANES), "band", split_axis=0, concat_axis=0, tiled=True)
    right_blocks = -(-HALO * sections // LANES)
    right = shifted(mine[:, : right_blocks * part], "tm", -1)
    left = shifted(mine[:, (blocks - 2) * part :], "tm", 1)

    best = pl.pallas_call(
        functools.partial(merge_kernel, sections, band_count),
        out_shape=jax.ShapeDtypeStruct((cols, rows), jnp.float32),
        in_specs=[pl.BlockSpec(memory_space=pltpu.SMEM)] + [pl.BlockSpec(memory_space=pltpu.VMEM)] * 3,
        out_specs=pl.BlockSpec(memory_space=pltpu.VMEM),
        scratch_shapes=[
            pltpu.VMEM((rows, SLOTS, LANES), jnp.float32),
            pltpu.VMEM((rows, SLOTS, LANES), jnp.float32),
            pltpu.VMEM((WMAX + cols, rows), jnp.float32),
        ],
        compiler_params=pltpu.CompilerParams(vmem_limit_bytes=32 * 2**20),
    )(shifts, *(piece.reshape(-1, LANES) for piece in (mine, right, left)))

    slabs = best.reshape(band_count, cols // band_count, rows)
    slabs = lax.all_to_all(slabs, "band", split_axis=0, concat_axis=0, tiled=True)
    return slabs.transpose(1, 0, 2).reshape(cols // band_count, band_count * rows).T


def solution(mesh):
    in_specs = (P("band", "tm"), P())
    out_specs = P(None, ("tm", "band"))
    return jax.shard_map(body, mesh=mesh, in_specs=in_specs, out_specs=out_specs, check_vma=False)
```

time: 1480 us -> 81.3 us (0.05)
  local copies, waits for them, and re-layouts: 1320 us -> 2.81 us
  starting transfers between devices: 73.5 us -> 14.3 us
  blocking collectives: 0 us -> 49.5 us
  waiting for transfers between devices: 52.9 us -> 5.9 us
  loops' own time: 15.5 us -> 0 us
    gather x2561 -> x0, local copies, waits for them, and re-layouts: 1310 us -> none
    all_to_all x0 -> x2, blocking collectives: none -> 49.5 us  [the longest x1 26.6 us: body(): lax.all_to_all(packed.reshape(band_count, part * blocks, LANES), 'band',...]
    ppermute x5 -> x0, waiting for transfers between devices: 28.7 us -> none  [partner(): return lax.ppermute(block, axis, route)]
    ppermute x6 -> x2, starting transfers between devices: 37.1 us -> 14.3 us  [shifted(): lax.ppermute(value, axis, [(source, source + steps) for source in range(i...]
    ppermute x5 -> x0, starting transfers between devices: 21.1 us -> none  [partner(): return lax.ppermute(block, axis, route)]
    all_to_all x1 -> x0, waiting for transfers between devices: 16.6 us -> none  [body(): lax.all_to_all(best_snr, 'band', split_axis=1, concat_axis=0, tiled=True)]
    another operation x5 -> x0, loops' own time: 15.5 us -> none  [one_row(): return lax.dynamic_slice_in_dim(single_row, row_shift, length, 0)]
    all_to_all x1 -> x0, starting transfers between devices: 15.3 us -> none  [body(): lax.all_to_all(best_snr, 'band', split_axis=1, concat_axis=0, tiled=True)]
  transfers between devices with their start and end apart: 12 -> 2, of which waited for: 12 -> 1; matrix products, arithmetic and copies ran while one was open for 0% -> 0% of each run, Pallas kernels for 0% -> 0%
where the time goes in v1:
time: 81.3 us; the launch traced here: 81.1 us
  blocking collectives  49.5 us (61%)
  starting transfers between devices  14.3 us (18%)
  Pallas kernels  8.51 us (10%)
  waiting for transfers between devices  5.9 us (7%)
  local copies, waits for them, and re-layouts  2.81 us (3%)
    all_to_all x1, blocking collectives, body(): lax.all_to_all(packed.reshape(band_count, part * blocks, LANES), 'band',...  26.6 us
    all_to_all x1, blocking collectives, body(): lax.all_to_all(slabs, 'band', split_axis=0, concat_axis=0, tiled=True)  23 us
    ppermute x2, starting transfers between devices, shifted(): lax.ppermute(value, axis, [(source, source + steps) for source in range(i...  14.3 us
    pallas_call x1, Pallas kernels, body(): pl.pallas_call(functools.partial(merge_kernel, sections, band_count), out...  8.34 us
    ppermute x2, waiting for transfers between devices, shifted(): lax.ppermute(value, axis, [(source, source + steps) for source in range(i...  5.9 us
    unnamed x4, local copies, waits for them, and re-layouts  1.94 us
  transfers between devices with their start and end apart: 2, of which 1 were waited for; matrix products, arithmetic and copies ran while one was open for 0% of the time, Pallas kernels for 0%

profile of v1, /device:TPU:9, one launch (start us, length us, event | category | flops | bytes accessed | tf_op | source)
XLA Modules:
  0.0 81.1 jit_solution(7292539521457917017)
XLA Ops:
  0.0 0.0 copy-start
  0.0 1.0 %copy-done = f32[128,1024]{1,0:T(8,128)S(1)} copy-done((f32[128,1024]{1,0:T(8,128)S(1)}, f32[128,1024]{1,0:T(8,128)}, u32[]{:S(2)}) %copy-start) | copy-done | bytes 524312
  1.0 0.0 copy-start.1
  1.0 0.9 %copy-done.1 = s32[5,4096]{1,0:T(8,128)S(1)} copy-done((s32[5,4096]{1,0:T(8,128)S(1)}, s32[5,4096]{1,0:T(8,128)}, u32[]{:S(2)}) %copy-start.1) | copy-done | bytes 81944
  1.9 0.2 shard_map.28
  2.1 26.6 %all_to_all.10 = f32[32,32,128]{2,1,0:T(8,128)S(1)} all-to-all(f32[32,32,128]{2,1,0:T(8,128)S(1)} %bitcast.15), channel_id=1, replica_groups=mesh['band'=32,'tm'=16] {'band'}, dimensions={0} | all-to-all | bytes 1048576 | tf_op jit(solution)/shard_map/all_to_all | solution.py:148
  28.7 12.3 %collective-permute-start = (f32[32,16,128]{2,1,0:T(8,128)S(1)}, f32[32,16,128]{2,1,0:T(8,128)S(1)}, u32[]{:S(2)}, u32[]{:S(2)}) collective-permute-start(f32[32,16,128]{2,1,0:T(8,128)S(1)} %slice.8), channel_id=1, source_target_pairs={{1,0},{2,1},{3,2},{4,3},{5,4},{6,5},{7,6},{8,7},{9,8},{10,9},{11,1... | collective-permute-start | bytes 786440 | tf_op jit(solution)/shard_map/ppermute | solution.py:20
  41.1 1.9 %collective-permute-start.1 = (f32[32,8,128]{2,1,0:T(8,128)S(1)}, f32[32,8,128]{2,1,0:T(8,128)S(1)}, u32[]{:S(2)}, u32[]{:S(2)}) collective-permute-start(f32[32,8,128]{2,1,0:T(8,128)S(1)} %slice.9), channel_id=1, source_target_pairs={{0,1},{1,2},{2,3},{3,4},{4,5},{5,6},{6,7},{7,8},{8,9},{9,10},{10,1... | collective-permute-start | bytes 393224 | tf_op jit(solution)/shard_map/ppermute | solution.py:20
  43.0 5.9 %collective-permute-done.1 = f32[32,8,128]{2,1,0:T(8,128)S(1)} collective-permute-done((f32[32,8,128]{2,1,0:T(8,128)S(1)}, f32[32,8,128]{2,1,0:T(8,128)S(1)}, u32[]{:S(2)}, u32[]{:S(2)}) %collective-permute-start.1) | collective-permute-done | bytes 131104 | tf_op jit(solution)/shard_map/ppermute | solution.py:20
  48.9 0.0 collective-permute-done
  48.9 8.3 %shard_map.29 = f32[1024,128]{1,0:T(8,128)S(1)} custom-call(s32[5,128]{1,0:T(8,128)S(1)} %get-tuple-element.7.delays_ref, f32[1024,128]{1,0:T(8,128)S(1)} %bitcast.13, f32[512,128]{1,0:T(8,128)S(1)} %bitcast.16, f32[256,128]{1,0:T(8,128)S(1)} %bitcast.17), custom_call_target="tpu_custom_call" | custom-call | tf_op jit(solution)/shard_map/pallas_call | solution.py:153
  57.2 23.0 %all_to_all.11 = f32[32,32,128]{2,1,0:T(8,128)S(1)} all-to-all(f32[32,32,128]{2,1,0:T(8,128)S(1)} %bitcast.14), channel_id=1, replica_groups=mesh['band'=32,'tm'=16] {'band'}, dimensions={0} | all-to-all | bytes 1048576 | tf_op jit(solution)/shard_map/all_to_all | solution.py:167
  80.2 0.8 %bitcast_bitcast_fusion = f32[4096,32]{0,1:T(8,128)} fusion(f32[32,32,128]{2,1,0:T(8,128)S(1)} %all_to_all.11), kind=kLoop, calls=%fused_computation | loop fusion | bytes 1048576 | tf_op jit(solution)/shard_map/transpose | solution.py:168
  (2 shorter events, 0.0 us)
Async XLA Ops:
  0.0 1.0 %copy-start = (f32[128,1024]{1,0:T(8,128)S(1)}, f32[128,1024]{1,0:T(8,128)}, u32[]{:S(2)}) copy-start(f32[128,1024]{1,0:T(8,128)} %x_ref.1) | copy-start | bytes 1572868
  1.0 0.9 %copy-start.1 = (s32[5,4096]{1,0:T(8,128)S(1)}, s32[5,4096]{1,0:T(8,128)}, u32[]{:S(2)}) copy-start(s32[5,4096]{1,0:T(8,128)} %delays_ref.1) | copy-start | bytes 245764
  28.7 20.2 %collective-permute-start = (f32[32,16,128]{2,1,0:T(8,128)S(1)}, f32[32,16,128]{2,1,0:T(8,128)S(1)}, u32[]{:S(2)}, u32[]{:S(2)}) collective-permute-start(f32[32,16,128]{2,1,0:T(8,128)S(1)} %slice.8), channel_id=1, source_target_pairs={{1,0},{2,1},{3,2},{4,3},{5,4},{6,5},{7,6},{8,7},{9,8},{10,9},{11,1... | collective-permute-start | bytes 786440 | tf_op jit(solution)/shard_map/ppermute | solution.py:20
  41.1 7.8 %collective-permute-start.1 = (f32[32,8,128]{2,1,0:T(8,128)S(1)}, f32[32,8,128]{2,1,0:T(8,128)S(1)}, u32[]{:S(2)}, u32[]{:S(2)}) collective-permute-start(f32[32,8,128]{2,1,0:T(8,128)S(1)} %slice.9), channel_id=1, source_target_pairs={{0,1},{1,2},{2,3},{3,4},{4,5},{5,6},{6,7},{7,8},{8,9},{9,10},{10,1... | collective-permute-start | bytes 393224 | tf_op jit(solution)/shard_map/ppermute | solution.py:20

commit v2 on v1

v2 whole, which is shorter than its diff:
```python
import functools
import math

import jax
import jax.numpy as jnp
from jax import lax
from jax.experimental import pallas as pl
from jax.experimental.pallas import tpu as pltpu
from jax.sharding import PartitionSpec as P

HALO = 96
WMAX = 64
LANES = 128
SLOTS = 16
VMEM = pl.BlockSpec(memory_space=pltpu.VMEM)
SMEM = pl.BlockSpec(memory_space=pltpu.SMEM)


def shifted(value, axis, steps):
    count = lax.axis_size(axis)
    initial, last = (max(0, -steps), min(count, count - steps))
    return lax.ppermute(value, axis, [(source, source + steps) for source in range(initial, last)])


def right_blocks(band_count):
    sections = band_count.bit_length() - 1
    return [-(-HALO * (sections - bin(band).count("1")) // LANES) for band in range(band_count)]


def pack_kernel(x_ref, out_ref):
    rows, cols = x_ref.shape
    blocks = cols // LANES
    for group in range(rows // 8):
        for block in range(blocks):
            out_ref[pl.ds(group * 8 * blocks + block, 8, stride=blocks), :] = x_ref[
                group * 8 : group * 8 + 8, block * LANES : (block + 1) * LANES
            ]


def delays_kernel(sections, band_count, part, delays_ref, shifts_ref):
    my_band = lax.axis_index("band")
    lane = lax.broadcasted_iota(jnp.int32, (1, LANES), 1)
    for section_idx in range(sections):
        group = 2 << section_idx
        span = part * group
        first = my_band * span
        line = jnp.zeros((1, LANES), jnp.int32)
        for merged in range(band_count // group):
            column = pl.multiple_of(merged * group * LANES + first // LANES * LANES, LANES)
            values = delays_ref[section_idx : section_idx + 1, pl.ds(column, LANES)]
            turn = lax.rem(merged * span - lax.rem(first, LANES) + LANES, LANES)
            values = pltpu.roll(values, turn, 1)
            line = jnp.where((lane >= merged * span) & (lane < (merged + 1) * span), values, line)
        shifts_ref[section_idx : section_idx + 1, :] = line


def rims_kernel(counts, part, blocks, main_ref, right_ref, left_ref):
    place = 0
    for row in range(len(counts) * part):
        count = counts[row // part]
        if count:
            right_ref[place : place + count, :] = main_ref[row * blocks : row * blocks + count, :]
        place += count
        left_ref[row : row + 1, :] = main_ref[row * blocks + blocks - 1 : row * blocks + blocks, :]


def merge_kernel(sections, counts, part, blocks, shifts_ref, main_ref, right_ref, left_ref, out_ref, *scratch):
    ping_a, ping_b, pong_a, pong_b, turned = scratch
    band_count = len(counts)
    rows = band_count * part
    time_len = blocks * LANES
    lane = lax.broadcasted_iota(jnp.int32, (8, LANES), 1)
    last_slot = lax.broadcasted_iota(jnp.int32, (8, LANES), 0) == 7

    place = 0
    for row in range(rows):
        count = counts[row // part]
        if count:
            ping_b[row * 8 : row * 8 + count, :] = right_ref[place : place + count, :]
        place += count
        ping_b[row * 8 + 7 : row * 8 + 8, :] = left_ref[row : row + 1, :]

    source, target = (main_ref, ping_b), (pong_a, pong_b)
    for section_idx in range(sections):
        half = part << section_idx
        for step in range(rows // 2):
            within = step % half
            base = (step - within) * 2
            lower = (base + within) * 8
            upper = lower + half * 8
            low_a = source[0][lower : lower + 8, :]
            low_b = source[1][lower : lower + 8, :]
            roll_a = pltpu.roll(low_a, 7, 0)
            roll_b = pltpu.roll(low_b, 7, 0)
            next_a = jnp.where(last_slot, roll_b, roll_a)
            next_b = jnp.where(last_slot, roll_a, roll_b)
            up_a = source[0][upper : upper + 8, :]
            up_b = source[1][upper : upper + 8, :]
            for side in range(2):
                row = base + within * 2 + side
                delay = shifts_ref[section_idx, row]
                turn = (LANES - delay) & (LANES - 1)
                own = lane >= delay
                target[0][row * 8 : row * 8 + 8, :] = up_a + pltpu.roll(jnp.where(own, low_a, next_a), turn, 1)
                target[1][row * 8 : row * 8 + 8, :] = up_b + pltpu.roll(jnp.where(own, low_b, next_b), turn, 1)
        source, target = target, ((ping_a, ping_b) if section_idx % 2 == 0 else (pong_a, pong_b))

    before = source[1][pl.ds(7, rows, stride=8), :].T
    turned[0:WMAX, :] = jnp.where(lax.axis_index("tm") > 0, before[LANES - WMAX :, :], 0.0)
    for block in range(blocks):
        turned[WMAX + block * LANES : WMAX + (block + 1) * LANES, :] = source[0][pl.ds(block, rows, stride=8), :].T

    for start in range(0, time_len, LANES):
        sums = turned[start : start + LANES + WMAX, :]
        best = sums[WMAX:, :] * (1.0 / math.sqrt(band_count))
        width = 1
        while width < WMAX:
            sums = sums + pltpu.roll(sums, width, 0)
            width *= 2
            best = jnp.maximum(best, sums[WMAX:, :] * (1.0 / math.sqrt(width * band_count)))
        out_ref[start : start + LANES, :] = best


def body(partial_sums, delays):
    band_count = lax.axis_size("band")
    sections = band_count.bit_length() - 1
    rows, cols = partial_sums.shape
    blocks = cols // LANES
    part = rows // band_count
    counts = right_blocks(band_count)
    params = pltpu.CompilerParams(vmem_limit_bytes=24 * 2**20)

    def struct(*shape, dtype=jnp.float32):
        return jax.ShapeDtypeStruct(shape, dtype)

    packed = pl.pallas_call(
        pack_kernel,
        out_shape=struct(rows * blocks, LANES),
        in_specs=[VMEM],
        out_specs=VMEM,
        compiler_params=params,
    )(partial_sums)
    shifts = pl.pallas_call(
        functools.partial(delays_kernel, sections, band_count, part),
        out_shape=struct(sections, LANES, dtype=jnp.int32),
        in_specs=[VMEM],
        out_specs=VMEM,
        compiler_params=params,
    )(delays)

    mine = lax.all_to_all(packed.reshape(band_count, part * blocks, LANES), "band", split_axis=0, concat_axis=0, tiled=True)
    mine = mine.reshape(rows * blocks, LANES)
    right, left = pl.pallas_call(
        functools.partial(rims_kernel, counts, part, blocks),
        out_shape=[struct(sum(counts) * part, LANES), struct(rows, LANES)],
        in_specs=[VMEM],
        out_specs=[VMEM] * 2,
        compiler_params=params,
    )(mine)
    right = shifted(right, "tm", -1)
    left = shifted(left, "tm", 1)

    best = pl.pallas_call(
        functools.partial(merge_kernel, sections, counts, part, blocks),
        out_shape=struct(cols, rows),
        in_specs=[SMEM] + [VMEM] * 3,
        out_specs=VMEM,
        scratch_shapes=[pltpu.VMEM((rows * 8, LANES), jnp.float32)] * 4 + [pltpu.VMEM((WMAX + cols, rows), jnp.float32)],
        compiler_params=params,
    )(shifts, mine, right, left)

    slabs = best.reshape(band_count, cols // band_count, rows)
    slabs = lax.all_to_all(slabs, "band", split_axis=0, concat_axis=0, tiled=True)
    return slabs.transpose(1, 0, 2).reshape(cols // band_count, band_count * rows).T


def solution(mesh):
    in_specs = (P("band", "tm"), P())
    out_specs = P(None, ("tm", "band"))
    return jax.shard_map(body, mesh=mesh, in_specs=in_specs, out_specs=out_specs, check_vma=False)
```

time: 81.3 us -> 73.8 us (0.908)
  Pallas kernels: 8.51 us -> 2.91 us
  local copies, waits for them, and re-layouts: 2.81 us -> 1.87 us
  waiting for transfers between devices: 5.9 us -> 5.02 us
    pallas_call x2 -> x4, Pallas kernels: 8.51 us -> 2.91 us  [the longest x1 2.58 us: body(): pl.pallas_call(functools.partial(merge_kernel, sections, counts, part, bl...]
    unnamed x4, local copies, waits for them, and re-layouts: 1.94 us -> 1.04 us
    ppermute x2, waiting for transfers between devices: 5.9 us -> 5.02 us  [shifted(): lax.ppermute(value, axis, [(source, source + steps) for source in range(i...]
where the time goes in v2:
time: 73.8 us; the launch traced here: 73.5 us
  blocking collectives  49.4 us (67%)
  starting transfers between devices  14.3 us (19%)
  waiting for transfers between devices  5.02 us (7%)
  Pallas kernels  2.91 us (4%)
  local copies, waits for them, and re-layouts  1.87 us (3%)
    all_to_all x1, blocking collectives, body(): lax.all_to_all(packed.reshape(band_count, part * blocks, LANES), 'band',...  26.6 us
    all_to_all x1, blocking collectives, body(): lax.all_to_all(slabs, 'band', split_axis=0, concat_axis=0, tiled=True)  22.8 us
    ppermute x2, starting transfers between devices, shifted(): lax.ppermute(value, axis, [(source, source + steps) for source in range(i...  14.3 us
    ppermute x2, waiting for transfers between devices, shifted(): lax.ppermute(value, axis, [(source, source + steps) for source in range(i...  5.02 us
    pallas_call x1, Pallas kernels, body(): pl.pallas_call(functools.partial(merge_kernel, sections, counts, part, bl...  2.58 us
  transfers between devices with their start and end apart: 2, of which 1 were waited for; matrix products, arithmetic and copies ran while one was open for 0% of the time, Pallas kernels for 0%

profile of v2, /device:TPU:9, one launch (start us, length us, event | category | flops | bytes accessed | tf_op | source)
XLA Modules:
  0.0 73.5 jit_solution(8904123881940972777)
XLA Ops:
  0.0 0.0 copy-start
  0.0 1.0 %copy-done = f32[128,1024]{1,0:T(8,128)S(1)} copy-done((f32[128,1024]{1,0:T(8,128)S(1)}, f32[128,1024]{1,0:T(8,128)}, u32[]{:S(2)}) %copy-start) | copy-done | bytes 524312
  1.0 0.1 shard_map.29
  1.1 26.6 %all_to_all.10 = f32[32,32,128]{2,1,0:T(8,128)S(1)} all-to-all(f32[32,32,128]{2,1,0:T(8,128)S(1)} %bitcast.14), channel_id=1, replica_groups=mesh['band'=32,'tm'=16] {'band'}, dimensions={0} | all-to-all | bytes 1048576 | tf_op jit(solution)/shard_map/all_to_all | solution.py:151
  27.7 0.0 copy-start.1
  27.7 0.1 shard_map.30
  27.8 12.3 %collective-permute-start = (f32[296,128]{1,0:T(8,128)S(1)}, f32[296,128]{1,0:T(8,128)S(1)}, u32[]{:S(2)}, u32[]{:S(2)}) collective-permute-start(f32[296,128]{1,0:T(8,128)S(1)} %get-tuple-element.7), channel_id=1, source_target_pairs={{1,0},{2,1},{3,2},{4,3},{5,4},{6,5},{7,6},{8,7},{9,8},{10,9},{11,1... | collective-permute-start | bytes 454664 | tf_op jit(solution)/shard_map/ppermute | solution.py:22
  40.1 1.9 %collective-permute-start.1 = (f32[128,128]{1,0:T(8,128)S(1)}, f32[128,128]{1,0:T(8,128)S(1)}, u32[]{:S(2)}, u32[]{:S(2)}) collective-permute-start(f32[128,128]{1,0:T(8,128)S(1)} %get-tuple-element.8), channel_id=1, source_target_pairs={{0,1},{1,2},{2,3},{3,4},{4,5},{5,6},{6,7},{7,8},{8,9},{9,10},{10,1... | collective-permute-start | bytes 196616 | tf_op jit(solution)/shard_map/ppermute | solution.py:22
  42.1 0.0 copy-done.1
  42.1 0.2 shard_map.28.shifts_ref
  42.2 5.0 %collective-permute-done.1.left_ref = f32[128,128]{1,0:T(8,128)S(1)} collective-permute-done((f32[128,128]{1,0:T(8,128)S(1)}, f32[128,128]{1,0:T(8,128)S(1)}, u32[]{:S(2)}, u32[]{:S(2)}) %collective-permute-start.1) | collective-permute-done | bytes 65568 | tf_op jit(solution)/shard_map/ppermute | solution.py:22
  47.3 0.0 collective-permute-done.right_ref
  47.3 2.6 %shard_map.31 = f32[1024,128]{1,0:T(8,128)S(1)} custom-call(s32[5,128]{1,0:T(8,128)S(1)} %shard_map.28.shifts_ref, f32[1024,128]{1,0:T(8,128)S(1)} %bitcast.12, f32[296,128]{1,0:T(8,128)S(1)} %collective-permute-done.right_ref, f32[128,128]{1,0:T(8,128)S(1)} %collective-permute-done.1.left_ref), custom_call_target="tpu_custom_call" | custom-call | tf_op jit(solution)/shard_map/pallas_call | solution.py:163
  49.8 22.8 %all_to_all.11 = f32[32,32,128]{2,1,0:T(8,128)S(1)} all-to-all(f32[32,32,128]{2,1,0:T(8,128)S(1)} %bitcast.13), channel_id=1, replica_groups=mesh['band'=32,'tm'=16] {'band'}, dimensions={0} | all-to-all | bytes 1048576 | tf_op jit(solution)/shard_map/all_to_all | solution.py:173
  72.7 0.8 %bitcast_bitcast_fusion = f32[4096,32]{0,1:T(8,128)} fusion(f32[32,32,128]{2,1,0:T(8,128)S(1)} %all_to_all.11), kind=kLoop, calls=%fused_computation | loop fusion | bytes 1048576 | tf_op jit(solution)/shard_map/transpose | solution.py:174
Async XLA Ops:
  0.0 1.0 %copy-start = (f32[128,1024]{1,0:T(8,128)S(1)}, f32[128,1024]{1,0:T(8,128)}, u32[]{:S(2)}) copy-start(f32[128,1024]{1,0:T(8,128)} %x_ref.1) | copy-start | bytes 1572868
  27.7 14.4 %copy-start.1 = (s32[5,4096]{1,0:T(8,128)S(1)}, s32[5,4096]{1,0:T(8,128)}, u32[]{:S(2)}) copy-start(s32[5,4096]{1,0:T(8,128)} %delays_ref.1) | copy-start | bytes 245764
  27.8 19.5 %collective-permute-start = (f32[296,128]{1,0:T(8,128)S(1)}, f32[296,128]{1,0:T(8,128)S(1)}, u32[]{:S(2)}, u32[]{:S(2)}) collective-permute-start(f32[296,128]{1,0:T(8,128)S(1)} %get-tuple-element.7), channel_id=1, source_target_pairs={{1,0},{2,1},{3,2},{4,3},{5,4},{6,5},{7,6},{8,7},{9,8},{10,9},{11,1... | collective-permute-start | bytes 454664 | tf_op jit(solution)/shard_map/ppermute | solution.py:22
  40.1 7.1 %collective-permute-start.1 = (f32[128,128]{1,0:T(8,128)S(1)}, f32[128,128]{1,0:T(8,128)S(1)}, u32[]{:S(2)}, u32[]{:S(2)}) collective-permute-start(f32[128,128]{1,0:T(8,128)S(1)} %get-tuple-element.8), channel_id=1, source_target_pairs={{0,1},{1,2},{2,3},{3,4},{4,5},{5,6},{6,7},{7,8},{8,9},{9,10},{10,1... | collective-permute-start | bytes 196616 | tf_op jit(solution)/shard_map/ppermute | solution.py:22

commit v3 on v2

--- a/solution.py
+++ b/solution.py
@@ -14,12 +14,6 @@
 SLOTS = 16
 VMEM = pl.BlockSpec(memory_space=pltpu.VMEM)
 SMEM = pl.BlockSpec(memory_space=pltpu.SMEM)
-
-
-def shifted(value, axis, steps):
-    count = lax.axis_size(axis)
-    initial, last = (max(0, -steps), min(count, count - steps))
-    return lax.ppermute(value, axis, [(source, source + steps) for source in range(initial, last)])
 
 
 def right_blocks(band_count):
@@ -54,17 +48,19 @@
         shifts_ref[section_idx : section_idx + 1, :] = line
 
 
-def rims_kernel(counts, part, blocks, main_ref, right_ref, left_ref):
+def rims_kernel(counts, part, blocks, main_ref, right_ref, left_ref, middle_ref):
     place = 0
     for row in range(len(counts) * part):
         count = counts[row // part]
         if count:
             right_ref[place : place + count, :] = main_ref[row * blocks : row * blocks + count, :]
         place += count
-        left_ref[row : row + 1, :] = main_ref[row * blocks + blocks - 1 : row * blocks + blocks, :]
+        last = main_ref[row * blocks + blocks - 1 : row * blocks + blocks, :]
+        left_ref[row : row + 1, :] = last
+        middle_ref[row : row + 1, :] = last
 
 
-def merge_kernel(sections, counts, part, blocks, shifts_ref, main_ref, right_ref, left_ref, out_ref, *scratch):
+def merge_kernel(sections, counts, part, blocks, shifts_ref, main_ref, right_ref, left_ref, middle_ref, out_ref, *scratch):
     ping_a, ping_b, pong_a, pong_b, turned = scratch
     band_count = len(counts)
     rows = band_count * part
@@ -78,7 +74,15 @@
         if count:
             ping_b[row * 8 : row * 8 + count, :] = right_ref[place : place + count, :]
         place += count
-        ping_b[row * 8 + 7 : row * 8 + 8, :] = left_ref[row : row + 1, :]
+
+    def gather(ref):
+        for row in range(rows):
+            ping_b[row * 8 + 7 : row * 8 + 8, :] = ref[row : row + 1, :]
+
+    beyond = lax.axis_index("tm") - lax.axis_size("tm") // 2
+    on_middle = (beyond == 0) | (beyond == 1)
+    pl.when(on_middle)(lambda: gather(middle_ref))
+    pl.when(jnp.logical_not(on_middle))(lambda: gather(left_ref))
 
     source, target = (main_ref, ping_b), (pong_a, pong_b)
     for section_idx in range(sections):
@@ -150,24 +154,28 @@
 
     mine = lax.all_to_all(packed.reshape(band_count, part * blocks, LANES), "band", split_axis=0, concat_axis=0, tiled=True)
     mine = mine.reshape(rows * blocks, LANES)
-    right, left = pl.pallas_call(
+    count = lax.axis_size("tm")
+    middle_at = count // 2
+    wide = sum(counts) * part
+    right, left, middle = pl.pallas_call(
         functools.partial(rims_kernel, counts, part, blocks),
-        out_shape=[struct(sum(counts) * part, LANES), struct(rows, LANES)],
+        out_shape=[struct(wide, LANES), struct(rows, LANES), struct(wide + 8, LANES)],
         in_specs=[VMEM],
-        out_specs=[VMEM] * 2,
+        out_specs=[VMEM] * 3,
         compiler_params=params,
     )(mine)
-    right = shifted(right, "tm", -1)
-    left = shifted(left, "tm", 1)
+    middle = lax.ppermute(middle, "tm", [(at - 1, at) for at in (middle_at, middle_at + 1)])
+    right = lax.ppermute(right, "tm", [(at, at - 1) for at in range(1, count)])
+    left = lax.ppermute(left, "tm", [(at - 1, at) for at in range(1, count) if at not in (middle_at, middle_at + 1)])
 
     best = pl.pallas_call(
         functools.partial(merge_kernel, sections, counts, part, blocks),
         out_shape=struct(cols, rows),
-        in_specs=[SMEM] + [VMEM] * 3,
+        in_specs=[SMEM] + [VMEM] * 4,
         out_specs=VMEM,
         scratch_shapes=[pltpu.VMEM((rows * 8, LANES), jnp.float32)] * 4 + [pltpu.VMEM((WMAX + cols, rows), jnp.float32)],
         compiler_params=params,
-    )(shifts, mine, right, left)
+    )(shifts, mine, right, left, middle)
 
     slabs = best.reshape(band_count, cols // band_count, rows)
     slabs = lax.all_to_all(slabs, "band", split_axis=0, concat_axis=0, tiled=True)

time: 73.8 us -> 70.2 us (0.951)
  waiting for transfers between devices: 5.02 us -> 1.27 us
    ppermute x2 -> x3, waiting for transfers between devices: 5.02 us -> 1.27 us  [the longest x1 1.26 us: body(): right = lax.ppermute(right, 'tm', [(at, at - 1) for at in range(1, count)])]
    ppermute x2 -> x3, starting transfers between devices: 14.3 us -> 14.3 us  [the longest x1 9.63 us: body(): right = lax.ppermute(right, 'tm', [(at, at - 1) for at in range(1, count)])]
  transfers between devices with their start and end apart: 2 -> 3, of which waited for: 1 -> 1; matrix products, arithmetic and copies ran while one was open for 0% -> 0% of each run, Pallas kernels for 0% -> 0%
where the time goes in v3:
time: 70.2 us; the launch traced here: 70 us
  blocking collectives  49.5 us (71%)
  starting transfers between devices  14.3 us (20%)
  Pallas kernels  3.01 us (4%)
  local copies, waits for them, and re-layouts  1.87 us (3%)
  waiting for transfers between devices  1.27 us (2%)
    all_to_all x1, blocking collectives, body(): lax.all_to_all(packed.reshape(band_count, part * blocks, LANES), 'band',...  26.6 us
    all_to_all x1, blocking collectives, body(): lax.all_to_all(slabs, 'band', split_axis=0, concat_axis=0, tiled=True)  22.9 us
    ppermute x1, starting transfers between devices, body(): right = lax.ppermute(right, 'tm', [(at, at - 1) for at in range(1, count)])  9.63 us
    ppermute x1, starting transfers between devices, body(): lax.ppermute(middle, 'tm', [(at - 1, at) for at in (middle_at, middle_at...  4 us
    pallas_call x1, Pallas kernels, body(): pl.pallas_call(functools.partial(merge_kernel, sections, counts, part, bl...  2.65 us
  transfers between devices with their start and end apart: 3, of which 1 were waited for; matrix products, arithmetic and copies ran while one was open for 0% of the time, Pallas kernels for 0%

profile of v3, /device:TPU:9, one launch (start us, length us, event | category | flops | bytes accessed | tf_op | source)
XLA Modules:
  0.0 70.0 jit_solution(8333079728061108712)
XLA Ops:
  0.0 0.0 copy-start
  0.0 1.0 %copy-done = f32[128,1024]{1,0:T(8,128)S(1)} copy-done((f32[128,1024]{1,0:T(8,128)S(1)}, f32[128,1024]{1,0:T(8,128)}, u32[]{:S(2)}) %copy-start) | copy-done | bytes 524312
  1.0 0.1 shard_map.29
  1.1 26.6 %all_to_all.10 = f32[32,32,128]{2,1,0:T(8,128)S(1)} all-to-all(f32[32,32,128]{2,1,0:T(8,128)S(1)} %bitcast.13), channel_id=1, replica_groups=mesh['band'=32,'tm'=16] {'band'}, dimensions={0} | all-to-all | bytes 1048576 | tf_op jit(solution)/shard_map/all_to_all | solution.py:155
  27.7 0.0 copy-start.1
  27.7 0.1 shard_map.30
  27.8 4.0 %collective-permute-start.2 = (f32[304,128]{1,0:T(8,128)S(1)}, f32[304,128]{1,0:T(8,128)S(1)}, u32[]{:S(2)}, u32[]{:S(2)}) collective-permute-start(f32[304,128]{1,0:T(8,128)S(1)} %get-tuple-element.10), channel_id=1, source_target_pairs={{7,8},{8,9},{23,24},{24,25},{39,40},{40,41},{55,56},{56,57},{71,72... | collective-permute-start | bytes 466952 | tf_op jit(solution)/shard_map/ppermute | solution.py:167
  31.8 9.6 %collective-permute-start = (f32[296,128]{1,0:T(8,128)S(1)}, f32[296,128]{1,0:T(8,128)S(1)}, u32[]{:S(2)}, u32[]{:S(2)}) collective-permute-start(f32[296,128]{1,0:T(8,128)S(1)} %get-tuple-element.8), channel_id=1, source_target_pairs={{1,0},{2,1},{3,2},{4,3},{5,4},{6,5},{7,6},{8,7},{9,8},{10,9},{11,1... | collective-permute-start | bytes 454664 | tf_op jit(solution)/shard_map/ppermute | solution.py:168
  41.5 0.7 collective-permute-start.1
  42.1 0.0 copy-done.1
  42.1 0.2 shard_map.28.shifts_ref
  42.3 0.0 collective-permute-done.1.left_ref
  42.3 1.3 %collective-permute-done.right_ref = f32[296,128]{1,0:T(8,128)S(1)} collective-permute-done((f32[296,128]{1,0:T(8,128)S(1)}, f32[296,128]{1,0:T(8,128)S(1)}, u32[]{:S(2)}, u32[]{:S(2)}) %collective-permute-start) | collective-permute-done | bytes 151584 | tf_op jit(solution)/shard_map/ppermute | solution.py:168
  43.6 0.0 collective-permute-done.2.middle_ref
  43.6 2.7 %shard_map.31 = f32[1024,128]{1,0:T(8,128)S(1)} custom-call(s32[5,128]{1,0:T(8,128)S(1)} %shard_map.28.shifts_ref, f32[1024,128]{1,0:T(8,128)S(1)} %bitcast.12, f32[296,128]{1,0:T(8,128)S(1)} %collective-permute-done.right_ref, f32[128,128]{1,0:T(8,128)S(1)} %collective-permute-done.1.left_ref, f32[304,128]{1,0:T(8,128)S(1)} %collective-permute-done.2.middle_ref), custom_call_target="tpu_custom_call" | custom-call | tf_op jit(solution)/shard_map/pallas_call | solution.py:171
  46.2 22.9 %all_to_all.11 = f32[32,32,128]{2,1,0:T(8,128)S(1)} all-to-all(f32[32,32,128]{2,1,0:T(8,128)S(1)} %bitcast.14), channel_id=1, replica_groups=mesh['band'=32,'tm'=16] {'band'}, dimensions={0} | all-to-all | bytes 1048576 | tf_op jit(solution)/shard_map/all_to_all | solution.py:181
  69.1 0.8 %bitcast_bitcast_fusion = f32[4096,32]{0,1:T(8,128)} fusion(f32[32,32,128]{2,1,0:T(8,128)S(1)} %all_to_all.11), kind=kLoop, calls=%fused_computation | loop fusion | bytes 1048576 | tf_op jit(solution)/shard_map/transpose | solution.py:182
Async XLA Ops:
  0.0 1.0 %copy-start = (f32[128,1024]{1,0:T(8,128)S(1)}, f32[128,1024]{1,0:T(8,128)}, u32[]{:S(2)}) copy-start(f32[128,1024]{1,0:T(8,128)} %x_ref.1) | copy-start | bytes 1572868
  27.7 14.4 %copy-start.1 = (s32[5,4096]{1,0:T(8,128)S(1)}, s32[5,4096]{1,0:T(8,128)}, u32[]{:S(2)}) copy-start(s32[5,4096]{1,0:T(8,128)} %delays_ref.1) | copy-start | bytes 245764
  27.8 15.8 %collective-permute-start.2 = (f32[304,128]{1,0:T(8,128)S(1)}, f32[304,128]{1,0:T(8,128)S(1)}, u32[]{:S(2)}, u32[]{:S(2)}) collective-permute-start(f32[304,128]{1,0:T(8,128)S(1)} %get-tuple-element.10), channel_id=1, source_target_pairs={{7,8},{8,9},{23,24},{24,25},{39,40},{40,41},{55,56},{56,57},{71,72... | collective-permute-start | bytes 466952 | tf_op jit(solution)/shard_map/ppermute | solution.py:167
  31.8 11.8 %collective-permute-start = (f32[296,128]{1,0:T(8,128)S(1)}, f32[296,128]{1,0:T(8,128)S(1)}, u32[]{:S(2)}, u32[]{:S(2)}) collective-permute-start(f32[296,128]{1,0:T(8,128)S(1)} %get-tuple-element.8), channel_id=1, source_target_pairs={{1,0},{2,1},{3,2},{4,3},{5,4},{6,5},{7,6},{8,7},{9,8},{10,9},{11,1... | collective-permute-start | bytes 454664 | tf_op jit(solution)/shard_map/ppermute | solution.py:168
  41.5 0.9 %collective-permute-start.1 = (f32[128,128]{1,0:T(8,128)S(1)}, f32[128,128]{1,0:T(8,128)S(1)}, u32[]{:S(2)}, u32[]{:S(2)}) collective-permute-start(f32[128,128]{1,0:T(8,128)S(1)} %get-tuple-element.9), channel_id=1, source_target_pairs={{0,1},{1,2},{2,3},{3,4},{4,5},{5,6},{6,7},{9,10},{10,11},{11,12},{... | collective-permute-start | bytes 196616 | tf_op jit(solution)/shard_map/ppermute | solution.py:169

commit v4 on v2

v4 whole, which is shorter than its diff:
```python
import functools
import math

import jax
import jax.numpy as jnp
from jax import lax
from jax.experimental import pallas as pl
from jax.experimental.pallas import tpu as pltpu
from jax.sharding import PartitionSpec as P

HALO = 96
WMAX = 64
LANES = 128
TILE = 8
VMEM = pl.BlockSpec(memory_space=pltpu.VMEM)
SMEM = pl.BlockSpec(memory_space=pltpu.SMEM)


def right_blocks(band_count):
    sections = band_count.bit_length() - 1
    return [-(-HALO * (sections - bin(band).count("1")) // LANES) for band in range(band_count)]


def pack_kernel(x_ref, out_ref):
    rows, cols = x_ref.shape
    blocks = cols // LANES
    for group in range(rows // 8):
        for block in range(blocks):
            out_ref[pl.ds(group * 8 * blocks + block, 8, stride=blocks), :] = x_ref[
                group * 8 : group * 8 + 8, block * LANES : (block + 1) * LANES
            ]


def pick_delays(sections, band_count, part, delays_ref, shifts_ref):
    my_band = lax.axis_index("band")
    lane = lax.broadcasted_iota(jnp.int32, (1, LANES), 1)
    for section_idx in range(sections):
        group = 2 << section_idx
        span = part * group
        first = my_band * span
        line = jnp.zeros((1, LANES), jnp.int32)
        for merged in range(band_count // group):
            column = pl.multiple_of(merged * group * LANES + first // LANES * LANES, LANES)
            values = delays_ref[section_idx : section_idx + 1, pl.ds(column, LANES)]
            turn = lax.rem(merged * span - lax.rem(first, LANES) + LANES, LANES)
            values = pltpu.roll(values, turn, 1)
            line = jnp.where((lane >= merged * span) & (lane < (merged + 1) * span), values, line)
        shifts_ref[section_idx : section_idx + 1, :] = line


def rims_kernel(counts, part, blocks, main_ref, delays_ref, right_ref, left_ref, middle_ref, shifts_ref):
    pick_delays(shifts_ref.shape[0], len(counts), part, delays_ref, shifts_ref)
    rows = len(counts) * part
    place = 0
    for row in range(rows):
        count = counts[row // part]
        if count:
            right_ref[place : place + count, :] = main_ref[row * blocks : row * blocks + count, :]
        place += count
    half = rows // 2
    low = main_ref[pl.ds(blocks - 1, half, stride=blocks), :]
    high = main_ref[pl.ds(half * blocks + blocks - 1, half, stride=blocks), :]
    lane = lax.broadcasted_iota(jnp.int32, (half, LANES), 1)
    both = jnp.where(lane < WMAX, pltpu.roll(low, WMAX, 1), high)
    left_ref[...] = both
    middle_ref[0:half, :] = both


def steps(rows, half):
    for step in range(rows // 2):
        within = step % half
        base = (step - within) * 2
        yield base + within, base + within + half, base + 2 * within


def inner_kernel(sections, band_count, part, blocks, shifts_ref, main_ref, out_ref, tail_ref, firsts_ref, ping, pong, turned):
    rows = band_count * part
    lane = lax.broadcasted_iota(jnp.int32, (TILE, LANES), 1)
    source, target = main_ref, pong
    for section_idx in range(sections):
        for lower, upper, row in steps(rows, part << section_idx):
            low = source[lower * TILE : (lower + 1) * TILE, :]
            later = pltpu.roll(low, TILE - 1, 0)
            up = source[upper * TILE : (upper + 1) * TILE, :]
            for side in range(2):
                at = row + side
                delay = shifts_ref[section_idx, at]
                turn = (LANES - delay) & (LANES - 1)
                merged = up + pltpu.roll(jnp.where(lane >= delay, low, later), turn, 1)
                target[at * TILE : (at + 1) * TILE, :] = merged
                if section_idx < sections - 1:
                    firsts_ref[section_idx * rows + at : section_idx * rows + at + 1, :] = merged[0:1, :]
        source, target = target, ping if section_idx % 2 == 0 else pong

    good = blocks // 2
    for block in range(good):
        turned[block * LANES : (block + 1) * LANES, :] = source[pl.ds(block, rows, stride=TILE), :].T
    tail_ref[0:LANES, :] = turned[0:LANES, :]
    tail_ref[LANES : LANES + WMAX, :] = turned[good * LANES - WMAX : good * LANES, :]
    for block in range(1, good):
        start = block * LANES
        sums = turned[start - WMAX : start + LANES, :]
        out_ref[start : start + LANES, :] = boxcars(sums, band_count)


def boxcars(sums, band_count):
    best = sums[WMAX:, :] * (1.0 / math.sqrt(band_count))
    width = 1
    while width < WMAX:
        sums = sums + pltpu.roll(sums, width, 0)
        width *= 2
        best = jnp.maximum(best, sums[WMAX:, :] * (1.0 / math.sqrt(width * band_count)))
    return best


def outer_kernel(sections, counts, part, blocks, *refs):
    shifts_ref, main_ref, right_ref, left_ref, middle_ref, tail_ref, firsts_ref, inner_ref, out_ref, ping, pong, turned = refs
    del inner_ref
    band_count = len(counts)
    rows = band_count * part
    good = blocks // 2
    lane = lax.broadcasted_iota(jnp.int32, (TILE, LANES), 1)
    slot = lax.broadcasted_iota(jnp.int32, (TILE, LANES), 0)

    places, place = [], 0
    for row in range(rows):
        count = counts[row // part]
        places.append(place)
        ping[row * TILE : row * TILE + good, :] = main_ref[row * blocks + good : (row + 1) * blocks, :]
        kept = min(count, TILE - 1 - good)
        if kept:
            ping[row * TILE + good : row * TILE + good + kept, :] = right_ref[place : place + kept, :]
        place += count

    beyond = lax.axis_index("tm") - lax.axis_size("tm") // 2
    from_left = jnp.where((beyond == 0) | (beyond == 1), middle_ref[0 : rows // 2, :], left_ref[...])
    ping[pl.ds(TILE - 1, rows // 2, stride=TILE), :] = pltpu.roll(from_left, WMAX, 1)
    ping[pl.ds(rows // 2 * TILE + TILE - 1, rows // 2, stride=TILE), :] = from_left

    source, target = ping, pong
    for section_idx in range(sections):
        for lower, upper, row in steps(rows, part << section_idx):
            low = source[lower * TILE : (lower + 1) * TILE, :]
            if section_idx == 0:
                first = main_ref[lower * blocks : lower * blocks + 1, :]
            else:
                at = (section_idx - 1) * rows + lower
                first = firsts_ref[at : at + 1, :]
            later = jnp.where(slot == TILE - 1, first, pltpu.roll(low, TILE - 1, 0))
            if section_idx == 0 and counts[lower // part] == TILE - good:
                fourth = places[lower] + TILE - good - 1
                later = jnp.where(slot == TILE - 2, right_ref[fourth : fourth + 1, :], later)
            up = source[upper * TILE : (upper + 1) * TILE, :]
            for side in range(2):
                at = row + side
                delay = shifts_ref[section_idx, at]
                turn = (LANES - delay) & (LANES - 1)
                target[at * TILE : (at + 1) * TILE, :] = up + pltpu.roll(jnp.where(lane >= delay, low, later), turn, 1)
        source, target = target, source

    before = source[pl.ds(TILE - 1, rows, stride=TILE), :].T[LANES - WMAX :, :]
    before = jnp.where(lax.axis_index("tm") > 0, before, 0.0)
    out_ref[0:LANES, :] = boxcars(jnp.concatenate([before, tail_ref[0:LANES, :]], axis=0), band_count)
    turned[0:WMAX, :] = tail_ref[LANES : LANES + WMAX, :]
    for block in range(blocks - good):
        turned[WMAX + block * LANES : WMAX + (block + 1) * LANES, :] = source[pl.ds(block, rows, stride=TILE), :].T
    for block in range(blocks - good):
        start = block * LANES
        place = (good + block) * LANES
        out_ref[place : place + LANES, :] = boxcars(turned[start : start + LANES + WMAX, :], band_count)


def body(partial_sums, delays):
    band_count = lax.axis_size("band")
    sections = band_count.bit_length() - 1
    rows, cols = partial_sums.shape
    blocks = cols // LANES
    part = rows // band_count
    counts = right_blocks(band_count)
    params = pltpu.CompilerParams(vmem_limit_bytes=24 * 2**20)

    def struct(*shape, dtype=jnp.float32):
        return jax.ShapeDtypeStruct(shape, dtype)

    def scratch(*shape):
        return pltpu.VMEM(shape, jnp.float32)

    packed = pl.pallas_call(
        pack_kernel,
        out_shape=struct(rows * blocks, LANES),
        in_specs=[VMEM],
        out_specs=VMEM,
        compiler_params=params,
    )(partial_sums)
    mine = lax.all_to_all(packed.reshape(band_count, part * blocks, LANES), "band", split_axis=0, concat_axis=0, tiled=True)
    mine = mine.reshape(rows * blocks, LANES)

    count = lax.axis_size("tm")
    middle_at = count // 2
    wide = sum(counts) * part
    right, left, middle, shifts = pl.pallas_call(
        functools.partial(rims_kernel, counts, part, blocks),
        out_shape=[
            struct(wide, LANES),
            struct(rows // 2, LANES),
            struct(wide + TILE, LANES),
            struct(sections, LANES, dtype=jnp.int32),
        ],
        in_specs=[VMEM] * 2,
        out_specs=[VMEM] * 4,
        compiler_params=params,
    )(mine, delays)

    middle = lax.ppermute(middle, "tm", [(at - 1, at) for at in (middle_at, middle_at + 1)])
    right = lax.ppermute(right, "tm", [(at, at - 1) for at in range(1, count)])
    left = lax.ppermute(left, "tm", [(at - 1, at) for at in range(1, count) if at not in (middle_at, middle_at + 1)])

    inner, tail, firsts = pl.pallas_call(
        functools.partial(inner_kernel, sections, band_count, part, blocks),
        out_shape=[struct(cols, rows), struct(LANES + WMAX, rows), struct((sections - 1) * rows, LANES)],
        in_specs=[SMEM, VMEM],
        out_specs=[VMEM] * 3,
        scratch_shapes=[scratch(rows * TILE, LANES), scratch(rows * TILE, LANES), scratch(cols // 2, rows)],
        compiler_params=params,
        cost_estimate=pl.CostEstimate(flops=2 * 10**6, bytes_accessed=4 * 2**20, transcendentals=0),
    )(shifts, mine)
    best = pl.pallas_call(
        functools.partial(outer_kernel, sections, counts, part, blocks),
        out_shape=struct(cols, rows),
        in_specs=[SMEM] + [VMEM] * 7,
        out_specs=VMEM,
        scratch_shapes=[scratch(rows * TILE, LANES), scratch(rows * TILE, LANES), scratch(WMAX + cols // 2, rows)],
        compiler_params=params,
        input_output_aliases={7: 0},
    )(shifts, mine, right, left, middle, tail, firsts, inner)

    slabs = best.reshape(band_count, cols // band_count, rows)
    slabs = lax.all_to_all(slabs, "band", split_axis=0, concat_axis=0, tiled=True)
    return slabs.transpose(1, 0, 2).reshape(cols // band_count, band_count * rows).T


def solution(mesh):
    in_specs = (P("band", "tm"), P())
    out_specs = P(None, ("tm", "band"))
    return jax.shard_map(body, mesh=mesh, in_specs=in_specs, out_specs=out_specs, check_vma=False)
```

time: 73.8 us -> 69.6 us (0.943)
  waiting for transfers between devices: 5.02 us -> 0.01 us
    ppermute x2 -> x3, waiting for transfers between devices: 5.02 us -> 0.01 us  [the longest x1 0.01 us: body(): lax.ppermute(middle, 'tm', [(at - 1, at) for at in (middle_at, middle_at...]
    ppermute x2 -> x3, starting transfers between devices: 14.3 us -> 14.3 us  [the longest x1 9.63 us: body(): right = lax.ppermute(right, 'tm', [(at, at - 1) for at in range(1, count)])]
  transfers between devices with their start and end apart: 2 -> 3, of which waited for: 1 -> 0; matrix products, arithmetic and copies ran while one was open for 0% -> 0% of each run, Pallas kernels for 0% -> 2%
where the time goes in v4:
time: 69.6 us; the launch traced here: 69.3 us
  blocking collectives  49.4 us (71%)
  starting transfers between devices  14.3 us (21%)
  Pallas kernels  3.62 us (5%)
  local copies, waits for them, and re-layouts  1.87 us (3%)
    all_to_all x1, blocking collectives, body(): lax.all_to_all(packed.reshape(band_count, part * blocks, LANES), 'band',...  26.7 us
    all_to_all x1, blocking collectives, body(): lax.all_to_all(slabs, 'band', split_axis=0, concat_axis=0, tiled=True)  22.7 us
    ppermute x1, starting transfers between devices, body(): right = lax.ppermute(right, 'tm', [(at, at - 1) for at in range(1, count)])  9.63 us
    ppermute x1, starting transfers between devices, body(): lax.ppermute(middle, 'tm', [(at - 1, at) for at in (middle_at, middle_at...  4 us
    pallas_call x1, Pallas kernels, body(): pl.pallas_call(functools.partial(outer_kernel, sections, counts, part, bl...  1.78 us
    pallas_call x1, Pallas kernels, body(): pl.pallas_call(functools.partial(inner_kernel, sections, band_count, part...  1.59 us
  transfers between devices with their start and end apart: 3, of which 0 were waited for; matrix products, arithmetic and copies ran while one was open for 0% of the time, Pallas kernels for 2%

profile of v4, /device:TPU:9, one launch (start us, length us, event | category | flops | bytes accessed | tf_op | source)
XLA Modules:
  0.0 69.3 jit_solution(9544288733560892434)
XLA Ops:
  0.0 0.0 copy-start
  0.0 1.0 %copy-done = f32[128,1024]{1,0:T(8,128)S(1)} copy-done((f32[128,1024]{1,0:T(8,128)S(1)}, f32[128,1024]{1,0:T(8,128)}, u32[]{:S(2)}) %copy-start) | copy-done | bytes 524312
  1.0 0.1 shard_map.28
  1.1 0.0 copy-start.1
  1.1 26.7 %all_to_all.10 = f32[32,32,128]{2,1,0:T(8,128)S(1)} all-to-all(f32[32,32,128]{2,1,0:T(8,128)S(1)} %bitcast.15), channel_id=1, replica_groups=mesh['band'=32,'tm'=16] {'band'}, dimensions={0} | all-to-all | bytes 1048576 | tf_op jit(solution)/shard_map/all_to_all | solution.py:195
  27.8 0.0 copy-done.1
  27.8 0.2 shard_map.29
  28.0 4.0 %collective-permute-start.2 = (f32[304,128]{1,0:T(8,128)S(1)}, f32[304,128]{1,0:T(8,128)S(1)}, u32[]{:S(2)}, u32[]{:S(2)}) collective-permute-start(f32[304,128]{1,0:T(8,128)S(1)} %get-tuple-element.15), channel_id=1, source_target_pairs={{7,8},{8,9},{23,24},{24,25},{39,40},{40,41},{55,56},{56,57},{71,72... | collective-permute-start | bytes 466952 | tf_op jit(solution)/shard_map/ppermute | solution.py:214
  32.0 9.6 %collective-permute-start = (f32[296,128]{1,0:T(8,128)S(1)}, f32[296,128]{1,0:T(8,128)S(1)}, u32[]{:S(2)}, u32[]{:S(2)}) collective-permute-start(f32[296,128]{1,0:T(8,128)S(1)} %get-tuple-element.13), channel_id=1, source_target_pairs={{1,0},{2,1},{3,2},{4,3},{5,4},{6,5},{7,6},{8,7},{9,8},{10,9},{11,1... | collective-permute-start | bytes 454664 | tf_op jit(solution)/shard_map/ppermute | solution.py:215
  41.7 0.7 collective-permute-start.1
  42.3 1.6 %shard_map.30 = (f32[1024,128]{1,0:T(8,128)S(1)}, f32[192,128]{1,0:T(8,128)S(1)}, f32[512,128]{1,0:T(8,128)S(1)}) custom-call(s32[5,128]{1,0:T(8,128)S(1)} %get-tuple-element.12.shifts_ref.refs_0_, f32[1024,128]{1,0:T(8,128)S(1)} %bitcast.12), custom_call_target="tpu_custom_call" | custom-call | flops 2000000 | bytes 4194304 | tf_op jit(solution)/shard_map/pallas_call | solution.py:218
  43.9 0.0 collective-permute-done.1.refs_3_
  43.9 0.0 collective-permute-done.refs_2_
  44.0 0.0 collective-permute-done.2.refs_4_
  44.0 1.8 %shard_map.31 = f32[1024,128]{1,0:T(8,128)S(1)} custom-call(s32[5,128]{1,0:T(8,128)S(1)} %get-tuple-element.12.shifts_ref.refs_0_, f32[1024,128]{1,0:T(8,128)S(1)} %bitcast.13, f32[296,128]{1,0:T(8,128)S(1)} %collective-permute-done.refs_2_, f32[64,128]{1,0:T(8,128)S(1)} %collective-permute-done.1.refs_3_, ...), custom_call_target="tpu_custom_call", output_to_operand_aliasing={{}: (7, {})} | custom-call | tf_op jit(solution)/shard_map/pallas_call | solution.py:227
  45.8 22.7 %all_to_all.11 = f32[32,32,128]{2,1,0:T(8,128)S(1)} all-to-all(f32[32,32,128]{2,1,0:T(8,128)S(1)} %bitcast.14), channel_id=1, replica_groups=mesh['band'=32,'tm'=16] {'band'}, dimensions={0} | all-to-all | bytes 1048576 | tf_op jit(solution)/shard_map/all_to_all | solution.py:238
  68.5 0.8 %bitcast_bitcast_fusion = f32[4096,32]{0,1:T(8,128)} fusion(f32[32,32,128]{2,1,0:T(8,128)S(1)} %all_to_all.11), kind=kLoop, calls=%fused_computation | loop fusion | bytes 1048576 | tf_op jit(solution)/shard_map/transpose | solution.py:239
Async XLA Ops:
  0.0 1.0 %copy-start = (f32[128,1024]{1,0:T(8,128)S(1)}, f32[128,1024]{1,0:T(8,128)}, u32[]{:S(2)}) copy-start(f32[128,1024]{1,0:T(8,128)} %x_ref.1) | copy-start | bytes 1572868
  1.1 26.7 %copy-start.1 = (s32[5,4096]{1,0:T(8,128)S(1)}, s32[5,4096]{1,0:T(8,128)}, u32[]{:S(2)}) copy-start(s32[5,4096]{1,0:T(8,128)} %delays_ref.1) | copy-start | bytes 245764
  28.0 15.9 %collective-permute-start.2 = (f32[304,128]{1,0:T(8,128)S(1)}, f32[304,128]{1,0:T(8,128)S(1)}, u32[]{:S(2)}, u32[]{:S(2)}) collective-permute-start(f32[304,128]{1,0:T(8,128)S(1)} %get-tuple-element.15), channel_id=1, source_target_pairs={{7,8},{8,9},{23,24},{24,25},{39,40},{40,41},{55,56},{56,57},{71,72... | collective-permute-start | bytes 466952 | tf_op jit(solution)/shard_map/ppermute | solution.py:214
  32.0 11.9 %collective-permute-start = (f32[296,128]{1,0:T(8,128)S(1)}, f32[296,128]{1,0:T(8,128)S(1)}, u32[]{:S(2)}, u32[]{:S(2)}) collective-permute-start(f32[296,128]{1,0:T(8,128)S(1)} %get-tuple-element.13), channel_id=1, source_target_pairs={{1,0},{2,1},{3,2},{4,3},{5,4},{6,5},{7,6},{8,7},{9,8},{10,9},{11,1... | collective-permute-start | bytes 454664 | tf_op jit(solution)/shard_map/ppermute | solution.py:215
  41.7 2.3 %collective-permute-start.1 = (f32[64,128]{1,0:T(8,128)S(1)}, f32[64,128]{1,0:T(8,128)S(1)}, u32[]{:S(2)}, u32[]{:S(2)}) collective-permute-start(f32[64,128]{1,0:T(8,128)S(1)} %get-tuple-element.14), channel_id=1, source_target_pairs={{0,1},{1,2},{2,3},{3,4},{4,5},{5,6},{6,7},{9,10},{10,11},{11,12},{... | collective-permute-start | bytes 98312 | tf_op jit(solution)/shard_map/ppermute | solution.py:216

commit v5 on v4

--- a/solution.py
+++ b/solution.py
@@ -13,12 +13,18 @@
 LANES = 128
 TILE = 8
 VMEM = pl.BlockSpec(memory_space=pltpu.VMEM)
-SMEM = pl.BlockSpec(memory_space=pltpu.SMEM)
 
 
 def right_blocks(band_count):
     sections = band_count.bit_length() - 1
-    return [-(-HALO * (sections - bin(band).count("1")) // LANES) for band in range(band_count)]
+    widths = [HALO * (sections - bin(band).count("1")) for band in range(band_count)]
+    return [
+        (width // LANES, width % LANES) if width % LANES <= LANES // 2 else (width // LANES + 1, 0) for width in widths
+    ]
+
+
+def right_rows(counts, part):
+    return sum(whole * part + left_over * part // LANES for whole, left_over in counts)
 
 
 def pack_kernel(x_ref, out_ref):
@@ -51,12 +57,22 @@
 def rims_kernel(counts, part, blocks, main_ref, delays_ref, right_ref, left_ref, middle_ref, shifts_ref):
     pick_delays(shifts_ref.shape[0], len(counts), part, delays_ref, shifts_ref)
     rows = len(counts) * part
+    one = lax.broadcasted_iota(jnp.int32, (1, LANES), 1)
     place = 0
-    for row in range(rows):
-        count = counts[row // part]
-        if count:
-            right_ref[place : place + count, :] = main_ref[row * blocks : row * blocks + count, :]
-        place += count
+    for band, (count, over) in enumerate(counts):
+        for row in range(band * part, (band + 1) * part):
+            if count:
+                right_ref[place : place + count, :] = main_ref[row * blocks : row * blocks + count, :]
+            place += count
+        share = LANES // over if over else part
+        for first in range(band * part, (band + 1) * part, share) if over else ():
+            line = main_ref[first * blocks + count : first * blocks + count + 1, :]
+            for index in range(1, share):
+                start = (first + index) * blocks + count
+                piece = pltpu.roll(main_ref[start : start + 1, :], index * over, 1)
+                line = jnp.where(one < index * over, line, piece)
+            right_ref[place : place + 1, :] = line
+            place += 1
     half = rows // 2
     low = main_ref[pl.ds(blocks - 1, half, stride=blocks), :]
     high = main_ref[pl.ds(half * blocks + blocks - 1, half, stride=blocks), :]
@@ -73,14 +89,22 @@
         yield base + within, base + within + half, base + 2 * within
 
 
-def inner_kernel(sections, band_count, part, blocks, shifts_ref, main_ref, out_ref, tail_ref, firsts_ref, ping, pong, turned):
+def inner_kernel(sections, band_count, part, blocks, table_ref, main_ref, out_ref, tail_ref, firsts_ref, outer_ref, *scratch):
+    ping, pong, turned, shifts_ref, sem = scratch
+    copy = pltpu.make_async_copy(table_ref, shifts_ref, sem)
+    copy.start()
     rows = band_count * part
+    good = blocks // 2
     lane = lax.broadcasted_iota(jnp.int32, (TILE, LANES), 1)
+    for row in range(rows):
+        outer_ref[row * TILE : row * TILE + good, :] = main_ref[row * blocks + good : (row + 1) * blocks, :]
+    copy.wait()
+
     source, target = main_ref, pong
     for section_idx in range(sections):
         for lower, upper, row in steps(rows, part << section_idx):
             low = source[lower * TILE : (lower + 1) * TILE, :]
-            later = pltpu.roll(low, TILE - 1, 0)
+            later = source[lower * TILE + 1 : (lower + 1) * TILE + 1, :]
             up = source[upper * TILE : (upper + 1) * TILE, :]
             for side in range(2):
                 at = row + side
@@ -92,7 +116,6 @@
                     firsts_ref[section_idx * rows + at : section_idx * rows + at + 1, :] = merged[0:1, :]
         source, target = target, ping if section_idx % 2 == 0 else pong
 
-    good = blocks // 2
     for block in range(good):
         turned[block * LANES : (block + 1) * LANES, :] = source[pl.ds(block, rows, stride=TILE), :].T
     tail_ref[0:LANES, :] = turned[0:LANES, :]
@@ -114,8 +137,10 @@
 
 
 def outer_kernel(sections, counts, part, blocks, *refs):
-    shifts_ref, main_ref, right_ref, left_ref, middle_ref, tail_ref, firsts_ref, inner_ref, out_ref, ping, pong, turned = refs
-    del inner_ref
+    table_ref, main_ref, right_ref, left_ref, middle_ref, tail_ref, firsts_ref = refs[:7]
+    out_ref, ping, pong, turned, shifts_ref, sem = refs[9:]
+    copy = pltpu.make_async_copy(table_ref, shifts_ref, sem)
+    copy.start()
     band_count = len(counts)
     rows = band_count * part
     good = blocks // 2
@@ -123,19 +148,27 @@
     slot = lax.broadcasted_iota(jnp.int32, (TILE, LANES), 0)
 
     places, place = [], 0
-    for row in range(rows):
-        count = counts[row // part]
-        places.append(place)
-        ping[row * TILE : row * TILE + good, :] = main_ref[row * blocks + good : (row + 1) * blocks, :]
+    for band, (count, over) in enumerate(counts):
         kept = min(count, TILE - 1 - good)
-        if kept:
-            ping[row * TILE + good : row * TILE + good + kept, :] = right_ref[place : place + kept, :]
-        place += count
+        for row in range(band * part, (band + 1) * part):
+            places.append(place)
+            if kept:
+                ping[row * TILE + good : row * TILE + good + kept, :] = right_ref[place : place + kept, :]
+            place += count
+        share = LANES // over if over else part
+        for row in range(band * part, (band + 1) * part) if over else ():
+            index = row % share
+            line = right_ref[place : place + 1, :]
+            if index:
+                line = pltpu.roll(line, LANES - index * over, 1)
+            ping[row * TILE + good + count : row * TILE + good + count + 1, :] = line
+            place += index == share - 1
 
     beyond = lax.axis_index("tm") - lax.axis_size("tm") // 2
     from_left = jnp.where((beyond == 0) | (beyond == 1), middle_ref[0 : rows // 2, :], left_ref[...])
     ping[pl.ds(TILE - 1, rows // 2, stride=TILE), :] = pltpu.roll(from_left, WMAX, 1)
     ping[pl.ds(rows // 2 * TILE + TILE - 1, rows // 2, stride=TILE), :] = from_left
+    copy.wait()
 
     source, target = ping, pong
     for section_idx in range(sections):
@@ -146,8 +179,8 @@
             else:
                 at = (section_idx - 1) * rows + lower
                 first = firsts_ref[at : at + 1, :]
-            later = jnp.where(slot == TILE - 1, first, pltpu.roll(low, TILE - 1, 0))
-            if section_idx == 0 and counts[lower // part] == TILE - good:
+            later = jnp.where(slot == TILE - 1, first, source[lower * TILE + 1 : (lower + 1) * TILE + 1, :])
+            if section_idx == 0 and counts[lower // part][0] == TILE - good:
                 fourth = places[lower] + TILE - good - 1
                 later = jnp.where(slot == TILE - 2, right_ref[fourth : fourth + 1, :], later)
             up = source[upper * TILE : (upper + 1) * TILE, :]
@@ -185,6 +218,8 @@
     def scratch(*shape):
         return pltpu.VMEM(shape, jnp.float32)
 
+    table = pltpu.SMEM((sections, LANES), jnp.int32)
+
     packed = pl.pallas_call(
         pack_kernel,
         out_shape=struct(rows * blocks, LANES),
@@ -197,7 +232,7 @@
 
     count = lax.axis_size("tm")
     middle_at = count // 2
-    wide = sum(counts) * part
+    wide = -(-right_rows(counts, part) // TILE) * TILE
     right, left, middle, shifts = pl.pallas_call(
         functools.partial(rims_kernel, counts, part, blocks),
         out_shape=[
@@ -215,24 +250,26 @@
     right = lax.ppermute(right, "tm", [(at, at - 1) for at in range(1, count)])
     left = lax.ppermute(left, "tm", [(at - 1, at) for at in range(1, count) if at not in (middle_at, middle_at + 1)])
 
-    inner, tail, firsts = pl.pallas_call(
+    merge_scratch = [scratch(rows * TILE, LANES), scratch(WMAX + cols // 2, rows), table, pltpu.SemaphoreType.DMA(())]
+    tile_rows = struct(rows * TILE, LANES)
+    inner, tail, firsts, outer = pl.pallas_call(
         functools.partial(inner_kernel, sections, band_count, part, blocks),
-        out_shape=[struct(cols, rows), struct(LANES + WMAX, rows), struct((sections - 1) * rows, LANES)],
-        in_specs=[SMEM, VMEM],
-        out_specs=[VMEM] * 3,
-        scratch_shapes=[scratch(rows * TILE, LANES), scratch(rows * TILE, LANES), scratch(cols // 2, rows)],
+        out_shape=[struct(cols, rows), struct(LANES + WMAX, rows), struct((sections - 1) * rows, LANES), tile_rows],
+        in_specs=[VMEM] * 2,
+        out_specs=[VMEM] * 4,
+        scratch_shapes=[scratch(rows * TILE, LANES)] + merge_scratch,
         compiler_params=params,
         cost_estimate=pl.CostEstimate(flops=2 * 10**6, bytes_accessed=4 * 2**20, transcendentals=0),
     )(shifts, mine)
-    best = pl.pallas_call(
+    best, _ = pl.pallas_call(
         functools.partial(outer_kernel, sections, counts, part, blocks),
-        out_shape=struct(cols, rows),
-        in_specs=[SMEM] + [VMEM] * 7,
-        out_specs=VMEM,
-        scratch_shapes=[scratch(rows * TILE, LANES), scratch(rows * TILE, LANES), scratch(WMAX + cols // 2, rows)],
-        compiler_params=params,
-        input_output_aliases={7: 0},
-    )(shifts, mine, right, left, middle, tail, firsts, inner)
+        out_shape=[struct(cols, rows), tile_rows],
+        in_specs=[VMEM] * 9,
+        out_specs=[VMEM] * 2,
+        scratch_shapes=merge_scratch,
+        compiler_params=params,
+        input_output_aliases={7: 0, 8: 1},
+    )(shifts, mine, right, left, middle, tail, firsts, inner, outer)
 
     slabs = best.reshape(band_count, cols // band_count, rows)
     slabs = lax.all_to_all(slabs, "band", split_axis=0, concat_axis=0, tiled=True)

time: 69.6 us -> 69 us (level)
  no operation moved by 1% of the time
where the time goes in v5:
time: 69 us; the launch traced here: 68.8 us
  blocking collectives  48.9 us (71%)
  starting transfers between devices  14.3 us (21%)
  Pallas kernels  3.62 us (5%)
  local copies, waits for them, and re-layouts  1.87 us (3%)
    all_to_all x1, blocking collectives, body(): lax.all_to_all(packed.reshape(band_count, part * blocks, LANES), 'band',...  26.7 us
    all_to_all x1, blocking collectives, body(): lax.all_to_all(slabs, 'band', split_axis=0, concat_axis=0, tiled=True)  22.2 us
    ppermute x1, starting transfers between devices, body(): right = lax.ppermute(right, 'tm', [(at, at - 1) for at in range(1, count)])  9.63 us
    ppermute x1, starting transfers between devices, body(): lax.ppermute(middle, 'tm', [(at - 1, at) for at in (middle_at, middle_at...  4 us
    pallas_call x1, Pallas kernels, body(): pl.pallas_call(functools.partial(outer_kernel, sections, counts, part, bl...  1.73 us
    pallas_call x1, Pallas kernels, body(): pl.pallas_call(functools.partial(inner_kernel, sections, band_count, part...  1.58 us
  transfers between devices with their start and end apart: 3, of which 0 were waited for; matrix products, arithmetic and copies ran while one was open for 0% of the time, Pallas kernels for 2%

profile of v5, /device:TPU:9, one launch (start us, length us, event | category | flops | bytes accessed | tf_op | source)
XLA Modules:
  0.0 68.8 jit_solution(12417702883703116558)
XLA Ops:
  0.0 0.0 copy-start
  0.0 1.0 %copy-done = f32[128,1024]{1,0:T(8,128)S(1)} copy-done((f32[128,1024]{1,0:T(8,128)S(1)}, f32[128,1024]{1,0:T(8,128)}, u32[]{:S(2)}) %copy-start) | copy-done | bytes 524312
  1.0 0.1 shard_map.28
  1.1 0.0 copy-start.1
  1.1 26.7 %all_to_all.10 = f32[32,32,128]{2,1,0:T(8,128)S(1)} all-to-all(f32[32,32,128]{2,1,0:T(8,128)S(1)} %bitcast.15), channel_id=1, replica_groups=mesh['band'=32,'tm'=16] {'band'}, dimensions={0} | all-to-all | bytes 1048576 | tf_op jit(solution)/shard_map/all_to_all | solution.py:230
  27.8 0.0 copy-done.1
  27.8 0.2 shard_map.29
  28.1 4.0 %collective-permute-start.2 = (f32[256,128]{1,0:T(8,128)S(1)}, f32[256,128]{1,0:T(8,128)S(1)}, u32[]{:S(2)}, u32[]{:S(2)}) collective-permute-start(f32[256,128]{1,0:T(8,128)S(1)} %get-tuple-element.17), channel_id=1, source_target_pairs={{7,8},{8,9},{23,24},{24,25},{39,40},{40,41},{55,56},{56,57},{71,72... | collective-permute-start | bytes 393224 | tf_op jit(solution)/shard_map/ppermute | solution.py:249
  32.1 9.6 %collective-permute-start = (f32[248,128]{1,0:T(8,128)S(1)}, f32[248,128]{1,0:T(8,128)S(1)}, u32[]{:S(2)}, u32[]{:S(2)}) collective-permute-start(f32[248,128]{1,0:T(8,128)S(1)} %get-tuple-element.15), channel_id=1, source_target_pairs={{1,0},{2,1},{3,2},{4,3},{5,4},{6,5},{7,6},{8,7},{9,8},{10,9},{11,1... | collective-permute-start | bytes 380936 | tf_op jit(solution)/shard_map/ppermute | solution.py:250
  41.7 0.7 collective-permute-start.1
  42.4 1.6 %shard_map.30 = (f32[1024,128]{1,0:T(8,128)S(1)}, f32[192,128]{1,0:T(8,128)S(1)}, f32[512,128]{1,0:T(8,128)S(1)}, f32[1024,128]{1,0:T(8,128)S(1)}) custom-call(s32[5,128]{1,0:T(8,128)S(1)} %get-tuple-element.14.table_ref.refs_0_, f32[1024,128]{1,0:T(8,128)S(1)} %bitcast.12), custom_call_target="tpu_custom_call" | custom-call | flops 2000000 | bytes 4194304 | tf_op jit(solution)/shard_map/pallas_call | solution.py:255
  44.0 0.0 collective-permute-done.1.refs_3_
  44.0 0.0 collective-permute-done.refs_2_
  44.0 0.0 collective-permute-done.2.refs_4_
  44.0 1.7 %shard_map.31 = (f32[1024,128]{1,0:T(8,128)S(1)}, f32[1024,128]{1,0:T(8,128)S(1)}) custom-call(s32[5,128]{1,0:T(8,128)S(1)} %get-tuple-element.14.table_ref.refs_0_, f32[1024,128]{1,0:T(8,128)S(1)} %bitcast.13, f32[248,128]{1,0:T(8,128)S(1)} %collective-permute-done.refs_2_, ...), custom_call_target="tpu_custom_call", output_to_operand_aliasing={{0}: (7, {}), {1}: (8, {})} | custom-call | tf_op jit(solution)/shard_map/pallas_call | solution.py:264
  45.8 22.2 %all_to_all.11 = f32[32,32,128]{2,1,0:T(8,128)S(1)} all-to-all(f32[32,32,128]{2,1,0:T(8,128)S(1)} %bitcast.14), channel_id=1, replica_groups=mesh['band'=32,'tm'=16] {'band'}, dimensions={0} | all-to-all | bytes 1048576 | tf_op jit(solution)/shard_map/all_to_all | solution.py:275
  68.0 0.8 %bitcast_bitcast_fusion = f32[4096,32]{0,1:T(8,128)} fusion(f32[32,32,128]{2,1,0:T(8,128)S(1)} %all_to_all.11), kind=kLoop, calls=%fused_computation | loop fusion | bytes 1048576 | tf_op jit(solution)/shard_map/transpose | solution.py:276
Async XLA Ops:
  0.0 1.0 %copy-start = (f32[128,1024]{1,0:T(8,128)S(1)}, f32[128,1024]{1,0:T(8,128)}, u32[]{:S(2)}) copy-start(f32[128,1024]{1,0:T(8,128)} %x_ref.1) | copy-start | bytes 1572868
  1.1 26.7 %copy-start.1 = (s32[5,4096]{1,0:T(8,128)S(1)}, s32[5,4096]{1,0:T(8,128)}, u32[]{:S(2)}) copy-start(s32[5,4096]{1,0:T(8,128)} %delays_ref.1) | copy-start | bytes 245764
  28.1 15.9 %collective-permute-start.2 = (f32[256,128]{1,0:T(8,128)S(1)}, f32[256,128]{1,0:T(8,128)S(1)}, u32[]{:S(2)}, u32[]{:S(2)}) collective-permute-start(f32[256,128]{1,0:T(8,128)S(1)} %get-tuple-element.17), channel_id=1, source_target_pairs={{7,8},{8,9},{23,24},{24,25},{39,40},{40,41},{55,56},{56,57},{71,72... | collective-permute-start | bytes 393224 | tf_op jit(solution)/shard_map/ppermute | solution.py:249
  32.1 11.9 %collective-permute-start = (f32[248,128]{1,0:T(8,128)S(1)}, f32[248,128]{1,0:T(8,128)S(1)}, u32[]{:S(2)}, u32[]{:S(2)}) collective-permute-start(f32[248,128]{1,0:T(8,128)S(1)} %get-tuple-element.15), channel_id=1, source_target_pairs={{1,0},{2,1},{3,2},{4,3},{5,4},{6,5},{7,6},{8,7},{9,8},{10,9},{11,1... | collective-permute-start | bytes 380936 | tf_op jit(solution)/shard_map/ppermute | solution.py:250
  41.7 2.3 %collective-permute-start.1 = (f32[64,128]{1,0:T(8,128)S(1)}, f32[64,128]{1,0:T(8,128)S(1)}, u32[]{:S(2)}, u32[]{:S(2)}) collective-permute-start(f32[64,128]{1,0:T(8,128)S(1)} %get-tuple-element.16), channel_id=1, source_target_pairs={{0,1},{1,2},{2,3},{3,4},{4,5},{5,6},{6,7},{9,10},{10,11},{11,12},{... | collective-permute-start | bytes 98312 | tf_op jit(solution)/shard_map/ppermute | solution.py:251

commit v6 on v5

--- a/solution.py
+++ b/solution.py
@@ -123,7 +123,7 @@
     for block in range(1, good):
         start = block * LANES
         sums = turned[start - WMAX : start + LANES, :]
-        out_ref[start : start + LANES, :] = boxcars(sums, band_count)
+        out_ref[start - LANES : start, :] = boxcars(sums, band_count)
 
 
 def boxcars(sums, band_count):
@@ -137,10 +137,12 @@
 
 
 def outer_kernel(sections, counts, part, blocks, *refs):
-    table_ref, main_ref, right_ref, left_ref, middle_ref, tail_ref, firsts_ref = refs[:7]
+    table_ref, main_ref, right_ref, left_ref, middle_ref, tail_ref, firsts_ref, inner_ref, outer_ref = refs[:9]
     out_ref, ping, pong, turned, shifts_ref, sem = refs[9:]
     copy = pltpu.make_async_copy(table_ref, shifts_ref, sem)
     copy.start()
+    out_ref[LANES : LANES + inner_ref.shape[0], :] = inner_ref[...]
+    ping[...] = outer_ref[...]
     band_count = len(counts)
     rows = band_count * part
     good = blocks // 2
@@ -254,21 +256,25 @@
     tile_rows = struct(rows * TILE, LANES)
     inner, tail, firsts, outer = pl.pallas_call(
         functools.partial(inner_kernel, sections, band_count, part, blocks),
-        out_shape=[struct(cols, rows), struct(LANES + WMAX, rows), struct((sections - 1) * rows, LANES), tile_rows],
+        out_shape=[
+            struct(cols // 2 - LANES, rows),
+            struct(LANES + WMAX, rows),
+            struct((sections - 1) * rows, LANES),
+            tile_rows,
+        ],
         in_specs=[VMEM] * 2,
         out_specs=[VMEM] * 4,
         scratch_shapes=[scratch(rows * TILE, LANES)] + merge_scratch,
         compiler_params=params,
         cost_estimate=pl.CostEstimate(flops=2 * 10**6, bytes_accessed=4 * 2**20, transcendentals=0),
     )(shifts, mine)
-    best, _ = pl.pallas_call(
+    best = pl.pallas_call(
         functools.partial(outer_kernel, sections, counts, part, blocks),
-        out_shape=[struct(cols, rows), tile_rows],
+        out_shape=struct(cols, rows),
         in_specs=[VMEM] * 9,
-        out_specs=[VMEM] * 2,
-        scratch_shapes=merge_scratch,
-        compiler_params=params,
-        input_output_aliases={7: 0, 8: 1},
+        out_specs=VMEM,
+        scratch_shapes=[scratch(rows * TILE, LANES)] + merge_scratch,
+        compiler_params=params,
     )(shifts, mine, right, left, middle, tail, firsts, inner, outer)
 
     slabs = best.reshape(band_count, cols // band_count, rows)

time: 69 us -> 69 us (level)
  no operation moved by 1% of the time
where the time goes in v6:
time: 69 us; the launch traced here: 68.8 us
  blocking collectives  48.9 us (71%)
  starting transfers between devices  14.3 us (21%)
  Pallas kernels  3.6 us (5%)
  local copies, waits for them, and re-layouts  1.87 us (3%)
    all_to_all x1, blocking collectives, body(): lax.all_to_all(packed.reshape(band_count, part * blocks, LANES), 'band',...  26.7 us
    all_to_all x1, blocking collectives, body(): lax.all_to_all(slabs, 'band', split_axis=0, concat_axis=0, tiled=True)  22.2 us
    ppermute x1, starting transfers between devices, body(): right = lax.ppermute(right, 'tm', [(at, at - 1) for at in range(1, count)])  9.63 us
    ppermute x1, starting transfers between devices, body(): lax.ppermute(middle, 'tm', [(at - 1, at) for at in (middle_at, middle_at...  4 us
    pallas_call x1, Pallas kernels, body(): pl.pallas_call(functools.partial(outer_kernel, sections, counts, part, bl...  1.71 us
    pallas_call x1, Pallas kernels, body(): pl.pallas_call(functools.partial(inner_kernel, sections, band_count, part...  1.58 us
  transfers between devices with their start and end apart: 3, of which 0 were waited for; matrix products, arithmetic and copies ran while one was open for 0% of the time, Pallas kernels for 2%

profile of v6, /device:TPU:9, one launch (start us, length us, event | category | flops | bytes accessed | tf_op | source)
XLA Modules:
  0.0 68.8 jit_solution(450474771126460790)
XLA Ops:
  0.0 0.0 copy-start
  0.0 1.0 %copy-done = f32[128,1024]{1,0:T(8,128)S(1)} copy-done((f32[128,1024]{1,0:T(8,128)S(1)}, f32[128,1024]{1,0:T(8,128)}, u32[]{:S(2)}) %copy-start) | copy-done | bytes 524312
  1.0 0.1 shard_map.28
  1.1 0.0 copy-start.1
  1.1 26.7 %all_to_all.10 = f32[32,32,128]{2,1,0:T(8,128)S(1)} all-to-all(f32[32,32,128]{2,1,0:T(8,128)S(1)} %bitcast.15), channel_id=1, replica_groups=mesh['band'=32,'tm'=16] {'band'}, dimensions={0} | all-to-all | bytes 1048576 | tf_op jit(solution)/shard_map/all_to_all | solution.py:232
  27.8 0.0 copy-done.1
  27.8 0.2 shard_map.29
  28.1 4.0 %collective-permute-start.2 = (f32[256,128]{1,0:T(8,128)S(1)}, f32[256,128]{1,0:T(8,128)S(1)}, u32[]{:S(2)}, u32[]{:S(2)}) collective-permute-start(f32[256,128]{1,0:T(8,128)S(1)} %get-tuple-element.16), channel_id=1, source_target_pairs={{7,8},{8,9},{23,24},{24,25},{39,40},{40,41},{55,56},{56,57},{71,72... | collective-permute-start | bytes 393224 | tf_op jit(solution)/shard_map/ppermute | solution.py:251
  32.1 9.6 %collective-permute-start = (f32[248,128]{1,0:T(8,128)S(1)}, f32[248,128]{1,0:T(8,128)S(1)}, u32[]{:S(2)}, u32[]{:S(2)}) collective-permute-start(f32[248,128]{1,0:T(8,128)S(1)} %get-tuple-element.14), channel_id=1, source_target_pairs={{1,0},{2,1},{3,2},{4,3},{5,4},{6,5},{7,6},{8,7},{9,8},{10,9},{11,1... | collective-permute-start | bytes 380936 | tf_op jit(solution)/shard_map/ppermute | solution.py:252
  41.7 0.7 collective-permute-start.1
  42.4 1.6 %shard_map.30 = (f32[384,128]{1,0:T(8,128)S(1)}, f32[192,128]{1,0:T(8,128)S(1)}, f32[512,128]{1,0:T(8,128)S(1)}, f32[1024,128]{1,0:T(8,128)S(1)}) custom-call(s32[5,128]{1,0:T(8,128)S(1)} %get-tuple-element.13.table_ref.refs_0_, f32[1024,128]{1,0:T(8,128)S(1)} %bitcast.12), custom_call_target="tpu_custom_call" | custom-call | flops 2000000 | bytes 4194304 | tf_op jit(solution)/shard_map/pallas_call | solution.py:257
  44.0 0.0 collective-permute-done.1.refs_3_
  44.0 0.0 collective-permute-done.refs_2_
  44.0 0.0 collective-permute-done.2.refs_4_
  44.0 1.7 %shard_map.31 = f32[1024,128]{1,0:T(8,128)S(1)} custom-call(s32[5,128]{1,0:T(8,128)S(1)} %get-tuple-element.13.table_ref.refs_0_, f32[1024,128]{1,0:T(8,128)S(1)} %bitcast.13, f32[248,128]{1,0:T(8,128)S(1)} %collective-permute-done.refs_2_, f32[64,128]{1,0:T(8,128)S(1)} %collective-permute-done.1.refs_3_, f32[256,128]{1,0:T(8,128)S(1)} %collective-permute-done.2.refs_4_, ...), custom_call_target="tpu_custom_call" | custom-call | tf_op jit(solution)/shard_map/pallas_call | solution.py:271
  45.7 22.2 %all_to_all.11 = f32[32,32,128]{2,1,0:T(8,128)S(1)} all-to-all(f32[32,32,128]{2,1,0:T(8,128)S(1)} %bitcast.14), channel_id=1, replica_groups=mesh['band'=32,'tm'=16] {'band'}, dimensions={0} | all-to-all | bytes 1048576 | tf_op jit(solution)/shard_map/all_to_all | solution.py:281
  67.9 0.8 %bitcast_bitcast_fusion = f32[4096,32]{0,1:T(8,128)} fusion(f32[32,32,128]{2,1,0:T(8,128)S(1)} %all_to_all.11), kind=kLoop, calls=%fused_computation | loop fusion | bytes 1048576 | tf_op jit(solution)/shard_map/transpose | solution.py:282
Async XLA Ops:
  0.0 1.0 %copy-start = (f32[128,1024]{1,0:T(8,128)S(1)}, f32[128,1024]{1,0:T(8,128)}, u32[]{:S(2)}) copy-start(f32[128,1024]{1,0:T(8,128)} %x_ref.1) | copy-start | bytes 1572868
  1.1 26.7 %copy-start.1 = (s32[5,4096]{1,0:T(8,128)S(1)}, s32[5,4096]{1,0:T(8,128)}, u32[]{:S(2)}) copy-start(s32[5,4096]{1,0:T(8,128)} %delays_ref.1) | copy-start | bytes 245764
  28.1 15.9 %collective-permute-start.2 = (f32[256,128]{1,0:T(8,128)S(1)}, f32[256,128]{1,0:T(8,128)S(1)}, u32[]{:S(2)}, u32[]{:S(2)}) collective-permute-start(f32[256,128]{1,0:T(8,128)S(1)} %get-tuple-element.16), channel_id=1, source_target_pairs={{7,8},{8,9},{23,24},{24,25},{39,40},{40,41},{55,56},{56,57},{71,72... | collective-permute-start | bytes 393224 | tf_op jit(solution)/shard_map/ppermute | solution.py:251
  32.1 11.9 %collective-permute-start = (f32[248,128]{1,0:T(8,128)S(1)}, f32[248,128]{1,0:T(8,128)S(1)}, u32[]{:S(2)}, u32[]{:S(2)}) collective-permute-start(f32[248,128]{1,0:T(8,128)S(1)} %get-tuple-element.14), channel_id=1, source_target_pairs={{1,0},{2,1},{3,2},{4,3},{5,4},{6,5},{7,6},{8,7},{9,8},{10,9},{11,1... | collective-permute-start | bytes 380936 | tf_op jit(solution)/shard_map/ppermute | solution.py:252
  41.7 2.3 %collective-permute-start.1 = (f32[64,128]{1,0:T(8,128)S(1)}, f32[64,128]{1,0:T(8,128)S(1)}, u32[]{:S(2)}, u32[]{:S(2)}) collective-permute-start(f32[64,128]{1,0:T(8,128)S(1)} %get-tuple-element.15), channel_id=1, source_target_pairs={{0,1},{1,2},{2,3},{3,4},{4,5},{5,6},{6,7},{9,10},{10,11},{11,12},{... | collective-permute-start | bytes 98312 | tf_op jit(solution)/shard_map/ppermute | solution.py:253

commit v7 on v6

--- a/solution.py
+++ b/solution.py
@@ -120,10 +120,7 @@
         turned[block * LANES : (block + 1) * LANES, :] = source[pl.ds(block, rows, stride=TILE), :].T
     tail_ref[0:LANES, :] = turned[0:LANES, :]
     tail_ref[LANES : LANES + WMAX, :] = turned[good * LANES - WMAX : good * LANES, :]
-    for block in range(1, good):
-        start = block * LANES
-        sums = turned[start - WMAX : start + LANES, :]
-        out_ref[start - LANES : start, :] = boxcars(sums, band_count)
+    stream(turned, LANES, (good - 1) * LANES, out_ref, 0, band_count)
 
 
 def boxcars(sums, band_count):
@@ -134,6 +131,31 @@
         width *= 2
         best = jnp.maximum(best, sums[WMAX:, :] * (1.0 / math.sqrt(width * band_count)))
     return best
+
+
+def stream(turned, start, length, out_ref, place, band_count):
+    index = lax.broadcasted_iota(jnp.int32, (TILE, LANES), 0)
+    turns, past = {}, []
+    for at in range(start - WMAX, start + length, TILE):
+        sums = turned[at : at + TILE, :]
+        best = sums * (1.0 / math.sqrt(band_count))
+        held = {}
+        width = 1
+        while width < WMAX:
+            held[width] = sums
+            if width < TILE:
+                turn = pltpu.roll(sums, width, 0)
+                earlier = jnp.where(index < width, turns.get(width, turn), turn)
+                turns[width] = turn
+            else:
+                back = width // TILE
+                earlier = past[-back][width] if len(past) >= back else sums
+            sums = sums + earlier
+            width *= 2
+            best = jnp.maximum(best, sums * (1.0 / math.sqrt(width * band_count)))
+        past.append(held)
+        if at >= start:
+            out_ref[place + at - start : place + at - start + TILE, :] = best
 
 
 def outer_kernel(sections, counts, part, blocks, *refs):
@@ -199,10 +221,7 @@
     turned[0:WMAX, :] = tail_ref[LANES : LANES + WMAX, :]
     for block in range(blocks - good):
         turned[WMAX + block * LANES : WMAX + (block + 1) * LANES, :] = source[pl.ds(block, rows, stride=TILE), :].T
-    for block in range(blocks - good):
-        start = block * LANES
-        place = (good + block) * LANES
-        out_ref[place : place + LANES, :] = boxcars(turned[start : start + LANES + WMAX, :], band_count)
+    stream(turned, WMAX, (blocks - good) * LANES, out_ref, good * LANES, band_count)
 
 
 def body(partial_sums, delays):

time: 69 us -> 69 us (level)
  no operation moved by 1% of the time
where the time goes in v7:
time: 69 us; the launch traced here: 68.7 us
  blocking collectives  48.9 us (71%)
  starting transfers between devices  14.3 us (21%)
  Pallas kernels  3.58 us (5%)
  local copies, waits for them, and re-layouts  1.87 us (3%)
    all_to_all x1, blocking collectives, body(): lax.all_to_all(packed.reshape(band_count, part * blocks, LANES), 'band',...  26.7 us
    all_to_all x1, blocking collectives, body(): lax.all_to_all(slabs, 'band', split_axis=0, concat_axis=0, tiled=True)  22.2 us
    ppermute x1, starting transfers between devices, body(): right = lax.ppermute(right, 'tm', [(at, at - 1) for at in range(1, count)])  9.63 us
    ppermute x1, starting transfers between devices, body(): lax.ppermute(middle, 'tm', [(at - 1, at) for at in (middle_at, middle_at...  4 us
    pallas_call x1, Pallas kernels, body(): pl.pallas_call(functools.partial(outer_kernel, sections, counts, part, bl...  1.69 us
    pallas_call x1, Pallas kernels, body(): pl.pallas_call(functools.partial(inner_kernel, sections, band_count, part...  1.58 us
  transfers between devices with their start and end apart: 3, of which 0 were waited for; matrix products, arithmetic and copies ran while one was open for 0% of the time, Pallas kernels for 2%

profile of v7, /device:TPU:9, one launch (start us, length us, event | category | flops | bytes accessed | tf_op | source)
XLA Modules:
  0.0 68.7 jit_solution(1284532661605197506)
XLA Ops:
  0.0 0.0 copy-start
  0.0 1.0 %copy-done = f32[128,1024]{1,0:T(8,128)S(1)} copy-done((f32[128,1024]{1,0:T(8,128)S(1)}, f32[128,1024]{1,0:T(8,128)}, u32[]{:S(2)}) %copy-start) | copy-done | bytes 524312
  1.0 0.1 shard_map.28
  1.1 0.0 copy-start.1
  1.1 26.7 %all_to_all.10 = f32[32,32,128]{2,1,0:T(8,128)S(1)} all-to-all(f32[32,32,128]{2,1,0:T(8,128)S(1)} %bitcast.15), channel_id=1, replica_groups=mesh['band'=32,'tm'=16] {'band'}, dimensions={0} | all-to-all | bytes 1048576 | tf_op jit(solution)/shard_map/all_to_all | solution.py:251
  27.8 0.0 copy-done.1
  27.8 0.2 shard_map.29
  28.1 4.0 %collective-permute-start.2 = (f32[256,128]{1,0:T(8,128)S(1)}, f32[256,128]{1,0:T(8,128)S(1)}, u32[]{:S(2)}, u32[]{:S(2)}) collective-permute-start(f32[256,128]{1,0:T(8,128)S(1)} %get-tuple-element.16), channel_id=1, source_target_pairs={{7,8},{8,9},{23,24},{24,25},{39,40},{40,41},{55,56},{56,57},{71,72... | collective-permute-start | bytes 393224 | tf_op jit(solution)/shard_map/ppermute | solution.py:270
  32.1 9.6 %collective-permute-start = (f32[248,128]{1,0:T(8,128)S(1)}, f32[248,128]{1,0:T(8,128)S(1)}, u32[]{:S(2)}, u32[]{:S(2)}) collective-permute-start(f32[248,128]{1,0:T(8,128)S(1)} %get-tuple-element.14), channel_id=1, source_target_pairs={{1,0},{2,1},{3,2},{4,3},{5,4},{6,5},{7,6},{8,7},{9,8},{10,9},{11,1... | collective-permute-start | bytes 380936 | tf_op jit(solution)/shard_map/ppermute | solution.py:271
  41.7 0.7 collective-permute-start.1
  42.4 1.6 %shard_map.30 = (f32[384,128]{1,0:T(8,128)S(1)}, f32[192,128]{1,0:T(8,128)S(1)}, f32[512,128]{1,0:T(8,128)S(1)}, f32[1024,128]{1,0:T(8,128)S(1)}) custom-call(s32[5,128]{1,0:T(8,128)S(1)} %get-tuple-element.13.table_ref.refs_0_, f32[1024,128]{1,0:T(8,128)S(1)} %bitcast.12), custom_call_target="tpu_custom_call" | custom-call | flops 2000000 | bytes 4194304 | tf_op jit(solution)/shard_map/pallas_call | solution.py:276
  44.0 0.0 collective-permute-done.1.refs_3_
  44.0 0.0 collective-permute-done.refs_2_
  44.0 0.0 collective-permute-done.2.refs_4_
  44.0 1.7 %shard_map.31 = f32[1024,128]{1,0:T(8,128)S(1)} custom-call(s32[5,128]{1,0:T(8,128)S(1)} %get-tuple-element.13.table_ref.refs_0_, f32[1024,128]{1,0:T(8,128)S(1)} %bitcast.13, f32[248,128]{1,0:T(8,128)S(1)} %collective-permute-done.refs_2_, f32[64,128]{1,0:T(8,128)S(1)} %collective-permute-done.1.refs_3_, f32[256,128]{1,0:T(8,128)S(1)} %collective-permute-done.2.refs_4_, ...), custom_call_target="tpu_custom_call" | custom-call | tf_op jit(solution)/shard_map/pallas_call | solution.py:290
  45.7 22.2 %all_to_all.11 = f32[32,32,128]{2,1,0:T(8,128)S(1)} all-to-all(f32[32,32,128]{2,1,0:T(8,128)S(1)} %bitcast.14), channel_id=1, replica_groups=mesh['band'=32,'tm'=16] {'band'}, dimensions={0} | all-to-all | bytes 1048576 | tf_op jit(solution)/shard_map/all_to_all | solution.py:300
  67.9 0.8 %bitcast_bitcast_fusion = f32[4096,32]{0,1:T(8,128)} fusion(f32[32,32,128]{2,1,0:T(8,128)S(1)} %all_to_all.11), kind=kLoop, calls=%fused_computation | loop fusion | bytes 1048576 | tf_op jit(solution)/shard_map/transpose | solution.py:301
Async XLA Ops:
  0.0 1.0 %copy-start = (f32[128,1024]{1,0:T(8,128)S(1)}, f32[128,1024]{1,0:T(8,128)}, u32[]{:S(2)}) copy-start(f32[128,1024]{1,0:T(8,128)} %x_ref.1) | copy-start | bytes 1572868
  1.1 26.7 %copy-start.1 = (s32[5,4096]{1,0:T(8,128)S(1)}, s32[5,4096]{1,0:T(8,128)}, u32[]{:S(2)}) copy-start(s32[5,4096]{1,0:T(8,128)} %delays_ref.1) | copy-start | bytes 245764
  28.1 15.9 %collective-permute-start.2 = (f32[256,128]{1,0:T(8,128)S(1)}, f32[256,128]{1,0:T(8,128)S(1)}, u32[]{:S(2)}, u32[]{:S(2)}) collective-permute-start(f32[256,128]{1,0:T(8,128)S(1)} %get-tuple-element.16), channel_id=1, source_target_pairs={{7,8},{8,9},{23,24},{24,25},{39,40},{40,41},{55,56},{56,57},{71,72... | collective-permute-start | bytes 393224 | tf_op jit(solution)/shard_map/ppermute | solution.py:270
  32.1 11.9 %collective-permute-start = (f32[248,128]{1,0:T(8,128)S(1)}, f32[248,128]{1,0:T(8,128)S(1)}, u32[]{:S(2)}, u32[]{:S(2)}) collective-permute-start(f32[248,128]{1,0:T(8,128)S(1)} %get-tuple-element.14), channel_id=1, source_target_pairs={{1,0},{2,1},{3,2},{4,3},{5,4},{6,5},{7,6},{8,7},{9,8},{10,9},{11,1... | collective-permute-start | bytes 380936 | tf_op jit(solution)/shard_map/ppermute | solution.py:271
  41.7 2.3 %collective-permute-start.1 = (f32[64,128]{1,0:T(8,128)S(1)}, f32[64,128]{1,0:T(8,128)S(1)}, u32[]{:S(2)}, u32[]{:S(2)}) collective-permute-start(f32[64,128]{1,0:T(8,128)S(1)} %get-tuple-element.15), channel_id=1, source_target_pairs={{0,1},{1,2},{2,3},{3,4},{4,5},{5,6},{6,7},{9,10},{10,11},{11,12},{... | collective-permute-start | bytes 98312 | tf_op jit(solution)/shard_map/ppermute | solution.py:272
